TPU v7x, 32 devices: a whole 2x2x4 slice. The times are simulated.
32 devices in a mesh: groups: 2 (over x), dp: 8 (over z, y), expert: 2 (over core).
Axes of the slice: x: 2, y: 2, z: 4, core: 2. Of those that a mesh axis runs over, the one named last changes fastest.
Arguments:
- tokens: bfloat16 [1024, 3072], P(('groups', 'expert')), parts along dimension 0, may hold values from -6 to 6
- router_weight: bfloat16 [3072, 4], replicated, may hold values from -0.109375 to 0.109375
- w_gate: bfloat16 [4, 3072, 16384], P('expert', None, 'dp'), may hold values from -0.109375 to 0.109375
- w_up: bfloat16 [4, 3072, 16384], P('expert', None, 'dp'), may hold values from -0.109375 to 0.109375
- w_down: bfloat16 [4, 16384, 3072], P('expert', 'dp'), may hold values from -0.046875 to 0.046875
- expert_ids: int32 [1024, 2], P(('groups', 'expert')), parts along dimension 0, may hold values from 0 to 3, all different within a row; in each aligned block of 256 rows (0 to 255, 256 to 511, ...) at most 192 rows name the same one
- positions: int32 [32], P('groups'), parts along dimension 0, may hold values from 0 to 511, as said below
- embed: float32 [32, 4096], P('groups'), parts along dimension 0, may hold values from -6 to 6
- w_first: float32 [3072, 4096], P(('dp', 'expert')), may hold values from -0.09375 to 0.09375
- w_second: float32 [3072, 3072], P(('dp', 'expert')), may hold values from -0.109375 to 0.109375
- cotangent: bfloat16 [32, 3072], P('groups'), parts along dimension 0, may hold values from -6 to 6
Outputs:
- mixed: bfloat16 [2, 512, 3072], P('expert', ('groups', 'dp')), parts along dimension 1
- grad_first: float32 [6144, 4096], P(('groups', 'dp', 'expert')), parts along dimension 0
- grad_second: float32 [6144, 3072], P(('groups', 'dp', 'expert')), parts along dimension 0
There are 2 independent parts, one for each index of `groups`. A program takes and returns all parts, laid end to end along the dimension named above; an argument that names none is the same for every part. Nothing has to cross between parts.
Inputs may be any that keep to these rules, and one draw needn't show every extreme that they name: `expert_ids`: within the 256 rows of one device no expert is named by more than 192 rows, and in some device's rows one expert is named by exactly 192; the two experts of a row differ. `positions`: 16 distinct token slots.
All inputs are finite; a program needn't handle non-finite values.
Results may differ from a plain program's by a relative error of at most 0.008.
Values may be sent and summed in bfloat16 or wider, within the bound.
A program may use at most 256 MiB of HBM per device.

v0:
```python
import jax
import jax.numpy as jnp
from jax import lax
from jax.sharding import PartitionSpec as P

EXPERTS = 4
TOP = 2
CAP = 192


PRECISE = lax.Precision.HIGHEST


def gelu_slope(values):
    normal_cdf = 0.5 * (1.0 + jax.scipy.special.erf(values * 0.7071067811865476))
    density = jnp.exp(-0.5 * values * values) * 0.3989422804014327
    return normal_cdf + values * density


def silu_slope(values):
    sigma = jax.nn.sigmoid(values)
    return sigma * (1.0 + values * (1.0 - sigma))


def gate_table(logits, mask):
    chosen_sum = jnp.sum(mask * logits, axis=1, keepdims=True)
    return mask * jax.nn.sigmoid(2.0 * logits - chosen_sum)


def expert_hidden(rows_in, w_gate, w_up, local):
    gate_pre = jnp.dot(rows_in, w_gate[local], preferred_element_type=jnp.float32)
    up_pre = jnp.dot(rows_in, w_up[local], preferred_element_type=jnp.float32)
    return (jax.nn.silu(gate_pre) * up_pre).astype(jnp.bfloat16)


def contract_last(left, right):
    return lax.dot_general(
        left, right, (((1,), (1,)), ((), ())), preferred_element_type=jnp.float32
    )


def body(
    tokens,
    router_weight,
    w_gate,
    w_up,
    w_down,
    expert_ids,
    positions,
    embed,
    w_first,
    w_second,
    cotangent,
):
    tok_rows, width = tokens.shape
    local_count = w_gate.shape[0]
    docs_count = positions.shape[0]
    halves = lax.axis_size("expert")
    dp_count = lax.axis_size("dp")
    out_rows = tok_rows // dp_count
    expert_base = lax.axis_index("expert") * local_count
    first_row = lax.axis_index("expert") * tok_rows
    row_index = first_row + jnp.arange(tok_rows, dtype=jnp.int32)
    expert_range = jnp.arange(EXPERTS, dtype=jnp.int32)
    choose = (expert_ids[:, :, None] == expert_range[None, None, :]).astype(jnp.float32)
    route_mask = jnp.sum(choose, axis=1)
    match = (row_index[:, None] == positions[None, :]).astype(jnp.float32)
    leading = (lax.axis_index("dp") == 0).astype(jnp.float32)
    pre_act = lax.dot_general(embed, w_first, (((1,), (1,)), ((), ())), precision=PRECISE)
    activated = jax.nn.gelu(pre_act, approximate=False)
    mask_part = leading * jnp.dot(match.T, route_mask, precision=PRECISE)
    projected, doc_mask = lax.psum(
        (jnp.dot(activated, w_second, precision=PRECISE), mask_part), ("dp", "expert")
    )
    doc_rows = projected.astype(jnp.bfloat16)
    placed = jnp.dot(match, projected, precision=PRECISE).astype(jnp.bfloat16)
    present = jnp.sum(match, axis=1, keepdims=True) > 0.5
    inputs = jnp.where(present, placed, tokens)
    logits = jnp.dot(inputs, router_weight, preferred_element_type=jnp.float32)
    gates = gate_table(logits, route_mask)
    flat_ids = expert_ids.reshape(-1)
    flat_hit = (flat_ids[:, None] == expert_range[None, :]).astype(jnp.int32)
    earlier = jnp.cumsum(flat_hit, axis=0) - flat_hit
    slot = jnp.sum(earlier * flat_hit, axis=1)
    target = flat_ids * CAP + slot
    source = jnp.repeat(jnp.arange(tok_rows, dtype=jnp.int32), TOP)
    slot_source = jnp.full((EXPERTS * CAP,), tok_rows, jnp.int32).at[target].set(source)
    padded = jnp.concatenate([inputs, jnp.zeros((1, width), jnp.bfloat16)], axis=0)
    outgoing = padded[slot_source].reshape(halves, local_count * CAP, width)
    arrived = lax.all_to_all(outgoing, "expert", split_axis=0, concat_axis=0, tiled=True)
    blocks = arrived.reshape(halves, local_count, CAP, width)
    out_parts = []
    for local in range(local_count):
        flat_rows = blocks[:, local].reshape(halves * CAP, width)
        hidden = expert_hidden(flat_rows, w_gate, w_up, local)
        out_parts.append(
            jnp.dot(hidden, w_down[local], preferred_element_type=jnp.float32).reshape(
                halves, CAP, width
            )
        )
    partial_slots = jnp.stack(out_parts, axis=1).reshape(halves, local_count * CAP, width)
    returned = (
        lax.all_to_all(
            partial_slots.astype(jnp.bfloat16), "expert", split_axis=0, concat_axis=0, tiled=True
        )
        .astype(partial_slots.dtype)
        .reshape(EXPERTS * CAP, width)
    )
    picked = returned[target].reshape(tok_rows, TOP, width)
    chosen_gate = jnp.take_along_axis(gates, expert_ids, axis=1)
    partial_mixed = jnp.sum(chosen_gate[:, :, None] * picked, axis=1)
    summed = lax.psum_scatter(partial_mixed, "dp", scatter_dimension=0, tiled=True)
    mixed = summed.astype(jnp.bfloat16).reshape(1, out_rows, width)
    doc_logits = jnp.dot(doc_rows, router_weight, preferred_element_type=jnp.float32)
    doc_gates = gate_table(doc_logits, doc_mask)
    own_doc_gates = lax.dynamic_slice_in_dim(doc_gates, expert_base, local_count, 1)
    cot_float = cotangent.astype(jnp.float32)
    expert_grad = jnp.zeros((docs_count, width), jnp.float32)
    score_list = []
    for local in range(local_count):
        gate_pre = jnp.dot(doc_rows, w_gate[local], preferred_element_type=jnp.float32)
        up_pre = jnp.dot(doc_rows, w_up[local], preferred_element_type=jnp.float32)
        sig_gate = jax.nn.silu(gate_pre)
        doc_hidden = (sig_gate * up_pre).astype(jnp.bfloat16)
        doc_out = jnp.dot(doc_hidden, w_down[local], preferred_element_type=jnp.float32)
        score_list.append(jnp.sum(cot_float * doc_out, axis=1))
        back_proj = contract_last(cotangent, w_down[local])
        scaled = own_doc_gates[:, local : local + 1] * back_proj
        up_grad = (scaled * sig_gate).astype(jnp.bfloat16)
        gate_grad = (scaled * up_pre * silu_slope(gate_pre)).astype(jnp.bfloat16)
        expert_grad = (
            expert_grad
            + contract_last(gate_grad, w_gate[local])
            + contract_last(up_grad, w_up[local])
        )
    score_local = jnp.stack(score_list, axis=1)
    score_part = lax.dynamic_update_slice_in_dim(
        jnp.zeros((docs_count, EXPERTS), jnp.float32), score_local, expert_base, 1
    )
    grad_sum, scores = lax.psum((expert_grad, score_part), ("dp", "expert"))
    centre = jnp.sum(doc_gates * scores, axis=1, keepdims=True)
    router_grad = doc_gates * (scores - centre)
    grad_proj = grad_sum + jnp.dot(
        router_grad, router_weight.astype(jnp.float32).T, precision=PRECISE
    )
    grad_second = jnp.dot(activated.T, grad_proj, precision=PRECISE)
    grad_hidden = lax.dot_general(
        grad_proj, w_second, (((1,), (1,)), ((), ())), precision=PRECISE
    ) * gelu_slope(pre_act)
    grad_first = jnp.dot(grad_hidden.T, embed, precision=PRECISE)
    return (mixed, grad_first, grad_second)


def solution(mesh):
    placed = (
        P(("groups", "expert"), None),
        P(),
        P("expert", None, "dp"),
        P("expert", None, "dp"),
        P("expert", "dp", None),
        P(("groups", "expert"), None),
        P("groups"),
        P("groups", None),
        P(("dp", "expert"), None),
        P(("dp", "expert"), None),
        P("groups", None),
    )
    return jax.shard_map(
        body,
        mesh=mesh,
        in_specs=placed,
        out_specs=(
            P("expert", ("groups", "dp"), None),
            P(("groups", "dp", "expert"), None),
            P(("groups", "dp", "expert"), None),
        ),
        check_vma=False,
    )
```

profile of v0, /device:TPU:0, one launch (start us, length us, event | category | flops | bytes accessed | tf_op | source)
XLA Modules:
  0.0 499.0 jit_solution(6547624293251211941)
XLA Ops:
  22.0 85.8 %all-reduce.5.cloned.1.call-done = f32[16,3072]{1,0:T(8,128)} async-done(((f32[16,3072]{1,0:T(8,128)}), f32[16,3072]{1,0:T(8,128)}) %all-reduce.5.cloned.1.call-update) | async-done | bytes 196624 | tf_op jit(solution)/shard_map/psum | solution.py:72
  108.8 6.3 %fusion.8 = f32[16,2048]{1,0:T(8,128)} fusion(bf16[16,3072]{1,0:T(8,128)(2,1)S(1)} %convert_element_type.68, bf16[2,3072,2048]{2,1,0:T(8,128)(2,1)} %param.14), kind=kOutput, calls=%fused_computation.12 | convolution fusion | flops 201326592 | bytes 12812288 | tf_op jit(solution)/shard_map/dot_general | solution.py:122
  115.2 6.9 %fusion.26 = f32[16,2048]{1,0:T(8,128)} fusion(bf16[16,3072]{1,0:T(8,128)(2,1)S(1)} %convert_element_type.68, bf16[2,3072,2048]{2,1,0:T(8,128)(2,1)} %param.14), kind=kOutput, calls=%fused_computation.30 | convolution fusion | flops 201326592 | bytes 12812288 | tf_op jit(solution)/shard_map/dot_general | solution.py:122
  137.1 9.4 %all_to_all.10 = bf16[2,384,3072]{2,1,0:T(8,128)(2,1)S(1)} all-to-all(bf16[2,384,3072]{2,1,0:T(8,128)(2,1)} %bitcast.154), channel_id=1, replica_groups=mesh['groups'=2,'dp'=8,'expert'=2] {'expert'}, dimensions={0} | all-to-all | bytes 9437184 | tf_op jit(solution)/shard_map/all_to_all | solution.py:90
  148.3 10.6 %fusion.16 = f32[384,2048]{1,0:T(8,128)} fusion(bf16[384,3072]{1,0:T(8,128)(2,1)} %bitcast.157, bf16[2,3072,2048]{2,1,0:T(8,128)(2,1)} %param.13), kind=kOutput, calls=%fused_computation.20 | convolution fusion | flops 4831838208 | bytes 18087936 | tf_op jit(solution)/shard_map/dot_general | solution.py:31
  161.3 8.7 %multiply_convert_fusion = bf16[384,2048]{1,0:T(8,128)(2,1)} fusion(f32[384,2048]{1,0:T(8,128)} %fusion.16, bf16[384,3072]{1,0:T(8,128)(2,1)} %bitcast.158, bf16[2,3072,2048]{2,1,0:T(8,128)(2,1)S(1)} %bitcast.151), kind=kOutput, calls=%fused_computation.73 | convolution fusion | flops 4836556800 | bytes 19660800 | tf_op jit(solution)/shard_map/dot_general | solution.py:32
  170.0 10.6 %fusion.34 = f32[384,2048]{1,0:T(8,128)} fusion(bf16[384,3072]{1,0:T(8,128)(2,1)S(1)} %bitcast.155, bf16[2,3072,2048]{2,1,0:T(8,128)(2,1)} %param.13), kind=kOutput, calls=%fused_computation.38 | convolution fusion | flops 4831838208 | bytes 18087936 | tf_op jit(solution)/shard_map/dot_general | solution.py:31
  180.6 9.8 %multiply_convert_fusion.1 = bf16[384,2048]{1,0:T(8,128)(2,1)} fusion(f32[384,2048]{1,0:T(8,128)} %fusion.34, bf16[384,3072]{1,0:T(8,128)(2,1)S(1)} %bitcast.156, bf16[2,3072,2048]{2,1,0:T(8,128)(2,1)} %param.14), kind=kOutput, calls=%fused_computation.74 | convolution fusion | flops 4836556800 | bytes 19660800 | tf_op jit(solution)/shard_map/dot_general | solution.py:32
  190.5 6.9 %fusion.60 = bf16[2,1,192,3072]{3,2,0,1:T(8,128)(2,1)S(1)} fusion(bf16[2,192,2048]{2,1,0:T(8,128)(2,1)} %bitcast.165, bf16[2,2048,3072]{2,1,0:T(8,128)(2,1)S(1)} %bitcast.149), kind=kOutput, calls=%fused_computation.63 | convolution fusion | flops 4833017856 | bytes 16515072 | tf_op jit(solution)/shard_map/dot_general | solution.py:97
  197.4 6.5 %fusion.63 = bf16[2,1,192,3072]{3,2,0,1:T(8,128)(2,1)} fusion(bf16[2,192,2048]{2,1,0:T(8,128)(2,1)S(1)} %bitcast.166, bf16[2,2048,3072]{2,1,0:T(8,128)(2,1)S(1)} %bitcast.149), kind=kOutput, calls=%fused_computation.64 | convolution fusion | flops 4833017856 | bytes 16515072 | tf_op jit(solution)/shard_map/dot_general | solution.py:97
  206.3 7.5 %all_to_all.11 = bf16[2,384,3072]{2,1,0:T(8,128)(2,1)S(1)} all-to-all(bf16[2,384,3072]{2,1,0:T(8,128)(2,1)S(1)} %bitcast.153), channel_id=1, replica_groups=mesh['groups'=2,'dp'=8,'expert'=2] {'expert'}, dimensions={0} | all-to-all | bytes 9437184 | tf_op jit(solution)/shard_map/all_to_all | solution.py:103
  219.1 10.9 %gather_fusion.1 = f32[512,3072]{1,0:T(8,128)} fusion(f32[768,3072]{1,0:T(8,128)} %bitcast_convert_fusion, s32[1024]{0:T(1024)S(1)} %pad_clamp_fusion), kind=kCustom, calls=%fused_computation.1 | custom fusion | bytes 12584960 | tf_op jit(solution)/shard_map/gather | solution.py:109
  230.0 8.2 %reshape.122 = f32[256,2,3072]{2,1,0:T(2,128)} reshape(f32[512,3072]{1,0:T(8,128)} %gather_fusion.1) | data formatting | bytes 12582912 | tf_op jit(solution)/shard_map/reshape | solution.py:109
  244.1 5.7 %fusion.92 = f32[16]{0:T(128)S(1)} fusion(bf16[2,2048,3072]{2,1,0:T(8,128)(2,1)} %param.15, bf16[16,3072]{1,0:T(8,128)(2,1)S(1)} %copy-done.11, f32[16,2048]{1,0:T(8,128)S(1)} %copy-done.15, f32[16,2048]{1,0:T(8,128)S(1)} %copy-done.14), kind=kOutput, calls=%fused_computation.77 | convolution fusion | flops 201670640 | bytes 12943424 | tf_op jit(solution)/shard_map/dot_general | solution.py:125
  255.6 31.7 %all-reduce.1 = (f32[16,4]{0,1:T(4,128)S(1)}, f32[16,4]{0,1:T(4,128)S(1)}) all-reduce(f32[16,4]{0,1:T(4,128)S(1)} %copy-done.22, f32[16,4]{0,1:T(4,128)S(1)} %maximum_dynamic-update-slice_fusion), channel_id=1, replica_groups=mesh['groups'=2,'dp'=8,'expert'=2] {'dp','expert'}, use_global_device_ids=true, to_apply=%region_10.11 | all-reduce | flops 128 | bytes 1024 | tf_op jit(solution)/shard_map/psum | solution.py:72
  287.6 6.3 %fusion.86 = f32[16,2048]{1,0:T(8,128)S(1)} fusion(bf16[16,3072]{1,0:T(8,128)(2,1)S(1)} %copy-done.11, bf16[2,2048,3072]{2,1,0:T(8,128)(2,1)} %param.15, f32[16]{0:T(128)S(1)} %get-tuple-element.10), kind=kOutput, calls=%fused_computation.75 | convolution fusion | flops 201359360 | bytes 12812352 | tf_op jit(solution)/shard_map/dot_general | solution.py:37
  293.9 6.3 %fusion.24 = f32[16,3072]{1,0:T(8,128)S(1)} fusion(bf16[2,3072,2048]{2,1,0:T(8,128)(2,1)} %param.14, f32[16,2048]{1,0:T(8,128)S(1)} %fusion.86, f32[16,2048]{1,0:T(8,128)S(1)} %copy-done.17), kind=kOutput, calls=%fused_computation.28 | convolution fusion | flops 201523200 | bytes 13041664 | tf_op jit(solution)/shard_map/dot_general | solution.py:37
  300.3 6.3 %fusion.67 = f32[16,3072]{1,0:T(8,128)S(1)} fusion(f32[16,3072]{1,0:T(8,128)S(1)} %fusion.24, bf16[2,3072,2048]{2,1,0:T(8,128)(2,1)} %param.13, f32[16,2048]{1,0:T(8,128)S(1)} %copy-done.17, f32[16,2048]{1,0:T(8,128)S(1)} %fusion.86, f32[16,2048]{1,0:T(8,128)S(1)} %copy-done.16), kind=kOutput, calls=%fused_computation.68 | convolution fusion | flops 201703424 | bytes 13369344 | tf_op jit(solution)/shard_map/dot_general | solution.py:37
  306.6 6.3 %fusion.89 = f32[16,2048]{1,0:T(8,128)S(1)} fusion(bf16[16,3072]{1,0:T(8,128)(2,1)S(1)} %copy-done.11, bf16[2,2048,3072]{2,1,0:T(8,128)(2,1)} %param.15, f32[16]{0:T(128)S(1)} %get-tuple-element.9), kind=kOutput, calls=%fused_computation.76 | convolution fusion | flops 201359360 | bytes 12812352 | tf_op jit(solution)/shard_map/dot_general | solution.py:37
  313.0 6.3 %fusion.73 = f32[16,3072]{1,0:T(8,128)S(1)} fusion(f32[16,3072]{1,0:T(8,128)S(1)} %fusion.67, bf16[2,3072,2048]{2,1,0:T(8,128)(2,1)} %param.13, f32[16,2048]{1,0:T(8,128)S(1)} %copy-done.14, f32[16,2048]{1,0:T(8,128)S(1)} %fusion.89, f32[16,2048]{1,0:T(8,128)S(1)} %copy-done.15), kind=kOutput, calls=%fused_computation.70 | convolution fusion | flops 201703424 | bytes 13369344 | tf_op jit(solution)/shard_map/dot_general | solution.py:37
  319.3 7.0 %fusion.76 = f32[16,3072]{1,0:T(8,128)} fusion(f32[16,3072]{1,0:T(8,128)S(1)} %fusion.73, bf16[2,3072,2048]{2,1,0:T(8,128)(2,1)} %param.14, f32[16,2048]{1,0:T(8,128)S(1)} %fusion.89, f32[16,2048]{1,0:T(8,128)S(1)} %copy-done.14), kind=kOutput, calls=%fused_computation.71 | convolution fusion | flops 201572352 | bytes 13238272 | tf_op jit(solution)/shard_map/dot_general | solution.py:37
  326.5 12.2 %multiply_reduce_fusion = f32[256,3072]{1,0:T(8,128)} fusion(f32[256,2,3072]{2,1,0:T(2,128)} %reshape.122, f32[256,2]{1,0:T(8,128)S(1)} %copy.37), kind=kLoop, calls=%fused_computation.58 | loop fusion | flops 2359296 | bytes 9439232 | tf_op jit(solution)/shard_map/reduce_sum | solution.py:111
  338.7 74.8 %all-reduce.7.cloned.1.call-done = f32[16,3072]{1,0:T(8,128)} async-done(((f32[16,3072]{1,0:T(8,128)}), f32[16,3072]{1,0:T(8,128)}) %all-reduce.7.cloned.1.call-update) | async-done | bytes 196624 | tf_op jit(solution)/shard_map/psum | solution.py:140
  426.3 64.2 %reduce-scatter.2.cloned.1.call-done = f32[32,3072]{1,0:T(8,128)} async-done(((f32[256,3072]{1,0:T(8,128)}), f32[32,3072]{1,0:T(8,128)}) %reduce-scatter.2.cloned.1.call-update) | async-done | bytes 393232 | tf_op jit(solution)/shard_map/reduce_scatter | solution.py:112
  (138 shorter events, 68.6 us)
Async XLA Ops:
  7.2 8.6 %copy-start.21 = (s32[16]{0:T(128)S(1)}, s32[16]{0:T(128)}, u32[]{:S(2)}) copy-start(s32[16]{0:T(128)} %param.17) | copy-start | bytes 196
  7.2 100.6 %all-reduce.5.cloned.1.call-start = ((), (), s32[]{:S(2)}) async-start(), calls=%async_computation.3 | async-start | bytes 393216 | tf_op jit(solution)/shard_map/psum | solution.py:72
  15.3 398.2 %all-reduce.7.cloned.1.call-start = ((), (), s32[]{:S(2)}) async-start(), calls=%async_computation.5 | async-start | bytes 393216 | tf_op jit(solution)/shard_map/psum | solution.py:140
  108.8 18.0 %copy-start.6 = (bf16[16,3072]{1,0:T(8,128)(2,1)}, bf16[16,3072]{1,0:T(8,128)(2,1)S(1)}, u32[]{:S(2)}) copy-start(bf16[16,3072]{1,0:T(8,128)(2,1)S(1)} %convert_element_type.68) | copy-start | bytes 294916
  108.8 15.5 %copy-start.2 = (bf16[2,3072,2048]{2,1,0:T(8,128)(2,1)S(1)}, bf16[2,3072,2048]{2,1,0:T(8,128)(2,1)}, u32[]{:S(2)}) copy-start(bf16[2,3072,2048]{2,1,0:T(8,128)(2,1)} %param.13) | copy-start | bytes 75497472
  146.6 12.4 %slice-start.6 = ((s8[25165824]{0:T(1024)(128)(4,1)}), s8[4194304]{0:T(1024)(128)(4,1)S(1)}, s32[]{:S(2)}) async-start(s8[25165824]{0:T(1024)(128)(4,1)} %bitcast.150), calls=%async_computation.12 | async-start | bytes 8388608
  146.6 12.4 %slice-start.7 = ((s8[25165824]{0:T(1024)(128)(4,1)}), s8[4194304]{0:T(1024)(128)(4,1)S(1)}, s32[]{:S(2)}) async-start(s8[25165824]{0:T(1024)(128)(4,1)} %bitcast.150), calls=%async_computation.13 | async-start | bytes 8388608
  148.3 10.7 %slice-start.8 = ((s8[25165824]{0:T(1024)(128)(4,1)}), s8[4194304]{0:T(1024)(128)(4,1)S(1)}, s32[]{:S(2)}) async-start(s8[25165824]{0:T(1024)(128)(4,1)} %bitcast.150), calls=%async_computation.14 | async-start | bytes 8388608
  148.3 10.7 %slice-start.9 = ((s8[25165824]{0:T(1024)(128)(4,1)}), s8[4194304]{0:T(1024)(128)(4,1)S(1)}, s32[]{:S(2)}) async-start(s8[25165824]{0:T(1024)(128)(4,1)} %bitcast.150), calls=%async_computation.15 | async-start | bytes 8388608
  148.3 11.8 %slice-start.10 = ((s8[25165824]{0:T(1024)(128)(4,1)}), s8[4194304]{0:T(1024)(128)(4,1)S(1)}, s32[]{:S(2)}) async-start(s8[25165824]{0:T(1024)(128)(4,1)} %bitcast.150), calls=%async_computation.16 | async-start | bytes 8388608
  148.3 13.0 %slice-start.11 = ((s8[25165824]{0:T(1024)(128)(4,1)}), s8[4194304]{0:T(1024)(128)(4,1)S(1)}, s32[]{:S(2)}) async-start(s8[25165824]{0:T(1024)(128)(4,1)} %bitcast.150), calls=%async_computation.17 | async-start | bytes 8388608
  170.0 20.4 %slice-start = ((s8[25165824]{0:T(1024)(128)(4,1)}), s8[4194304]{0:T(1024)(128)(4,1)S(1)}, s32[]{:S(2)}) async-start(s8[25165824]{0:T(1024)(128)(4,1)} %bitcast.148), calls=%async_computation.6 | async-start | bytes 8388608
  170.0 20.4 %slice-start.1 = ((s8[25165824]{0:T(1024)(128)(4,1)}), s8[4194304]{0:T(1024)(128)(4,1)S(1)}, s32[]{:S(2)}) async-start(s8[25165824]{0:T(1024)(128)(4,1)} %bitcast.148), calls=%async_computation.7 | async-start | bytes 8388608
  170.0 20.4 %slice-start.2 = ((s8[25165824]{0:T(1024)(128)(4,1)}), s8[4194304]{0:T(1024)(128)(4,1)S(1)}, s32[]{:S(2)}) async-start(s8[25165824]{0:T(1024)(128)(4,1)} %bitcast.148), calls=%async_computation.8 | async-start | bytes 8388608
  180.6 9.8 %slice-start.3 = ((s8[25165824]{0:T(1024)(128)(4,1)}), s8[4194304]{0:T(1024)(128)(4,1)S(1)}, s32[]{:S(2)}) async-start(s8[25165824]{0:T(1024)(128)(4,1)} %bitcast.148), calls=%async_computation.9 | async-start | bytes 8388608
  180.6 9.8 %slice-start.4 = ((s8[25165824]{0:T(1024)(128)(4,1)}), s8[4194304]{0:T(1024)(128)(4,1)S(1)}, s32[]{:S(2)}) async-start(s8[25165824]{0:T(1024)(128)(4,1)} %bitcast.148), calls=%async_computation.10 | async-start | bytes 8388608
  180.6 9.8 %slice-start.5 = ((s8[25165824]{0:T(1024)(128)(4,1)}), s8[4194304]{0:T(1024)(128)(4,1)S(1)}, s32[]{:S(2)}) async-start(s8[25165824]{0:T(1024)(128)(4,1)} %bitcast.148), calls=%async_computation.11 | async-start | bytes 8388608
  230.0 8.2 %copy-start.4 = (bf16[256,3072]{1,0:T(8,128)(2,1)S(1)}, bf16[256,3072]{1,0:T(8,128)(2,1)}, u32[]{:S(2)}) copy-start(bf16[256,3072]{1,0:T(8,128)(2,1)} %copy-done.3) | copy-start | bytes 4718596
  230.0 8.2 %copy-start.18 = (bf16[3072,4]{0,1:T(4,128)(2,1)S(1)}, bf16[3072,4]{0,1:T(4,128)(2,1)}, u32[]{:S(2)}) copy-start(bf16[3072,4]{0,1:T(4,128)(2,1)} %param.12) | copy-start | bytes 73732
  249.9 37.5 %copy-start.7 = (bf16[16,3072]{1,0:T(8,128)(2,1)S(1)}, bf16[16,3072]{1,0:T(8,128)(2,1)}, u32[]{:S(2)}) copy-start(bf16[16,3072]{1,0:T(8,128)(2,1)} %copy-done.6) | copy-start | bytes 294916
  326.4 88.5 %copy-start.13 = (f32[16,192]{1,0:T(8,128)S(1)}, f32[16,192]{1,0:T(8,128)}, u32[]{:S(2)}) copy-start(f32[16,192]{1,0:T(8,128)} %copy-done.12) | copy-start | bytes 36868
  326.4 164.1 %reduce-scatter.2.cloned.1.call-start = ((), (), s32[]{:S(2)}) async-start(), calls=%async_computation.4 | async-start | bytes 3538944 | tf_op jit(solution)/shard_map/reduce_scatter | solution.py:112
  338.7 83.3 %copy-start.9 = (f32[16,4096]{1,0:T(8,128)S(1)}, f32[16,4096]{1,0:T(8,128)}, u32[]{:S(2)}) copy-start(f32[16,4096]{1,0:T(8,128)} %param.18) | copy-start | bytes 786436
  413.5 78.7 %copy-start.1 = (f32[192,4096]{1,0:T(8,128)S(1)}, f32[192,4096]{1,0:T(8,128)}, u32[]{:S(2)}) copy-start(f32[192,4096]{1,0:T(8,128)} %param.19) | copy-start | bytes 9437188
  (15 other events, 66.2 us)
Sparse Core Ops, SparseCore 0:
  15.4 92.3 all-reduce.4
  326.5 86.9 all-reduce.6
  417.0 73.4 reduce-scatter.1
where the time goes:
time: 504 us; the launch traced here: 499 us
  waiting for transfers between devices  225 us (45%)
  matrix products  143 us (28%)
  blocking collectives  48.7 us (10%)
  local copies, waits for them, and re-layouts  43.8 us (9%)
  other arithmetic  23.9 us (5%)
  between operations  14.6 us (3%)
    psum x1, waiting for transfers between devices, body(): lax.psum((jnp.dot(activated, w_second, precision=PRECISE), mask_part), ('...  85.8 us
    psum x1, waiting for transfers between devices, body(): grad_sum, scores = lax.psum((expert_grad, score_part), ('dp', 'expert'))  74.8 us
    reduce_scatter x1, waiting for transfers between devices, body(): lax.psum_scatter(partial_mixed, 'dp', scatter_dimension=0, tiled=True)  64.2 us
    dot_general x6, matrix products, contract_last(): lax.dot_general(left, right, (((1,), (1,)), ((), ())), preferred_element_...  38.8 us
    psum x1, blocking collectives, body(): lax.psum((jnp.dot(activated, w_second, precision=PRECISE), mask_part), ('...  31.7 us
    dot_general x2, matrix products, expert_hidden(): jnp.dot(rows_in, w_gate[local], preferred_element_type=jnp.float32)  21.2 us
    dot_general x2, matrix products, expert_hidden(): up_pre = jnp.dot(rows_in, w_up[local], preferred_element_type=jnp.float32)  18.5 us
    dot_general x2, matrix products, body(): jnp.dot(hidden, w_down[local], preferred_element_type=jnp.float32)  13.4 us
  transfers between devices with their start and end apart: 3, of which 3 were waited for; matrix products, arithmetic and copies ran while one was open for 6% of the time, Pallas kernels for 0%

commit v1 on v0

v1 whole, which is shorter than its diff:
```python
import functools

import jax
import jax.numpy as jnp
from jax import lax
from jax.experimental import pallas as pl
from jax.experimental.pallas import tpu as pltpu
from jax.sharding import PartitionSpec as P

EXPERTS = 4
PRECISE = lax.Precision.HIGHEST
LANES = 128
FF_TILE = 512
VMEM_BYTES = 60 * 1024 * 1024


def gelu_slope(values):
    normal_cdf = 0.5 * (1.0 + jax.scipy.special.erf(values * 0.7071067811865476))
    density = jnp.exp(-0.5 * values * values) * 0.3989422804014327
    return normal_cdf + values * density


def gate_table(logits, mask):
    chosen_sum = jnp.sum(mask * logits, axis=1, keepdims=True)
    return mask * jax.nn.sigmoid(2.0 * logits - chosen_sum)


def contract_last(left, right):
    return lax.dot_general(
        left, right, (((1,), (1,)), ((), ())), preferred_element_type=jnp.float32
    )


def sum_kernel(dp_count, halves, x_ref, out_ref, land, total, sems):
    count = dp_count * halves
    me = lax.axis_index("dp") * halves + lax.axis_index("expert")

    def place(step):
        other = lax.rem(me + step, count)
        return other, {"dp": other // halves, "expert": lax.rem(other, halves)}

    barrier = pltpu.get_barrier_semaphore()
    for step in range(1, count):
        pl.semaphore_signal(
            barrier, inc=1, device_id=place(step)[1], device_id_type=pl.DeviceIdType.MESH
        )
    pl.semaphore_wait(barrier, count - 1)

    def scatter(step):
        other, device = place(step)
        return pltpu.make_async_remote_copy(
            src_ref=x_ref.at[other],
            dst_ref=land.at[step],
            send_sem=sems.at[0, step],
            recv_sem=sems.at[1, step],
            device_id=device,
            device_id_type=pl.DeviceIdType.MESH,
        )

    def spread(step):
        return pltpu.make_async_remote_copy(
            src_ref=total.at[me],
            dst_ref=total.at[me],
            send_sem=sems.at[2, step],
            recv_sem=sems.at[3, step],
            device_id=place(step)[1],
            device_id_type=pl.DeviceIdType.MESH,
        )

    for step in range(1, count):
        scatter(step).start()
    acc = x_ref[me]
    for step in range(1, count):
        scatter(step).wait_recv()
        acc = acc + land[step]
    total[me] = acc
    for step in range(1, count):
        spread(step).start()
    for step in range(1, count):
        scatter(step).wait_send()
    for step in range(1, count):
        spread(step).wait()
    out_ref[...] = total[...]


def sum_all(x, collective_id):
    dp_count = lax.axis_size("dp")
    halves = lax.axis_size("expert")
    count = dp_count * halves
    rows = x.shape[1]
    return pl.pallas_call(
        functools.partial(sum_kernel, dp_count, halves),
        out_shape=jax.ShapeDtypeStruct(x.shape, x.dtype),
        in_specs=[pl.BlockSpec(memory_space=pltpu.VMEM)],
        out_specs=pl.BlockSpec(memory_space=pltpu.VMEM),
        scratch_shapes=[
            pltpu.VMEM((count, rows, LANES), x.dtype),
            pltpu.VMEM((count, rows, LANES), x.dtype),
            pltpu.SemaphoreType.DMA((4, count)),
        ],
        compiler_params=pltpu.CompilerParams(
            collective_id=collective_id, has_side_effects=True
        ),
    )(x)


def expert_kernel(
    tok_count,
    rows_ref,
    gates_ref,
    doc_gates_ref,
    cot_ref,
    w_gate_ref,
    w_up_ref,
    w_down_ref,
    mixed_ref,
    grad_ref,
    score_ref,
):
    first = (pl.program_id(0) == 0) & (pl.program_id(1) == 0)

    @pl.when(first)
    def _():
        mixed_ref[...] = jnp.zeros_like(mixed_ref)
        grad_ref[...] = jnp.zeros_like(grad_ref)

    @pl.when(pl.program_id(1) == 0)
    def _():
        score_ref[...] = jnp.zeros_like(score_ref)

    rows = rows_ref[...]
    w_gate = w_gate_ref[0]
    w_up = w_up_ref[0]
    w_down = w_down_ref[0]
    gate_pre = jnp.dot(rows, w_gate, preferred_element_type=jnp.float32)
    up_pre = jnp.dot(rows, w_up, preferred_element_type=jnp.float32)
    sigma = jax.nn.sigmoid(gate_pre)
    silu = gate_pre * sigma
    product = silu * up_pre
    hidden = (product[:tok_count] * gates_ref[0]).astype(jnp.bfloat16)
    mixed_ref[...] += jnp.dot(hidden, w_down, preferred_element_type=jnp.float32)
    doc_gate = gate_pre[tok_count:]
    doc_up = up_pre[tok_count:]
    doc_sigma = sigma[tok_count:]
    doc_silu = silu[tok_count:]
    doc_hidden = product[tok_count:].astype(jnp.bfloat16).astype(jnp.float32)
    back = contract_last(cot_ref[...], w_down)
    score = jnp.sum(doc_hidden * back, axis=1, keepdims=True)
    score_ref[0] += jnp.broadcast_to(score, score_ref.shape[1:])
    scaled = back * doc_gates_ref[0]
    up_grad = (scaled * doc_silu).astype(jnp.bfloat16)
    slope = doc_sigma * (1.0 + doc_gate * (1.0 - doc_sigma))
    gate_grad = (scaled * doc_up * slope).astype(jnp.bfloat16)
    grad_ref[...] += contract_last(gate_grad, w_gate) + contract_last(up_grad, w_up)


def run_experts(rows, gates, doc_gates, cotangent, w_gate, w_up, w_down):
    local_count, width, ff = w_gate.shape
    tok_count = gates.shape[1]
    docs_count = cotangent.shape[0]
    tile = min(FF_TILE, ff)
    fixed = lambda e, f: (0, 0)
    of_expert = lambda e, f: (e, 0, 0)
    return pl.pallas_call(
        functools.partial(expert_kernel, tok_count),
        grid=(local_count, ff // tile),
        out_shape=(
            jax.ShapeDtypeStruct((tok_count, width), jnp.float32),
            jax.ShapeDtypeStruct((docs_count, width), jnp.float32),
            jax.ShapeDtypeStruct((local_count, docs_count, LANES), jnp.float32),
        ),
        in_specs=[
            pl.BlockSpec(rows.shape, fixed),
            pl.BlockSpec((1, tok_count, 1), of_expert),
            pl.BlockSpec((1, docs_count, 1), of_expert),
            pl.BlockSpec(cotangent.shape, fixed),
            pl.BlockSpec((1, width, tile), lambda e, f: (e, 0, f)),
            pl.BlockSpec((1, width, tile), lambda e, f: (e, 0, f)),
            pl.BlockSpec((1, tile, width), lambda e, f: (e, f, 0)),
        ],
        out_specs=(
            pl.BlockSpec((tok_count, width), fixed),
            pl.BlockSpec((docs_count, width), fixed),
            pl.BlockSpec((1, docs_count, LANES), of_expert),
        ),
        compiler_params=pltpu.CompilerParams(vmem_limit_bytes=VMEM_BYTES),
    )(rows, gates, doc_gates, cotangent, w_gate, w_up, w_down)


def body(
    tokens,
    router_weight,
    w_gate,
    w_up,
    w_down,
    expert_ids,
    positions,
    embed,
    w_first,
    w_second,
    cotangent,
):
    tok_rows, width = tokens.shape
    local_count = w_gate.shape[0]
    docs_count = positions.shape[0]
    halves = lax.axis_size("expert")
    dp_count = lax.axis_size("dp")
    count = halves * dp_count
    out_rows = tok_rows // dp_count
    half = lax.axis_index("expert")
    expert_base = half * local_count
    swap = [(0, 1), (1, 0)]

    all_tokens = jnp.concatenate([tokens, lax.ppermute(tokens, "expert", swap)], axis=0)
    all_ids = jnp.concatenate([expert_ids, lax.ppermute(expert_ids, "expert", swap)], axis=0)
    span = jnp.arange(tok_rows, dtype=jnp.int32)
    row_index = jnp.concatenate([half * tok_rows + span, (1 - half) * tok_rows + span])
    expert_range = jnp.arange(EXPERTS, dtype=jnp.int32)
    choose = (all_ids[:, :, None] == expert_range[None, None, :]).astype(jnp.float32)
    route_mask = jnp.sum(choose, axis=1)
    match = (row_index[:, None] == positions[None, :]).astype(jnp.float32)
    doc_mask = jnp.dot(match.T, route_mask, precision=PRECISE)

    pre_act = lax.dot_general(embed, w_first, (((1,), (1,)), ((), ())), precision=PRECISE)
    activated = jax.nn.gelu(pre_act, approximate=False)
    partial = jnp.dot(activated, w_second, precision=PRECISE)
    projected = sum_all(partial.reshape(count, -1, LANES), 1).reshape(docs_count, width)
    doc_rows = projected.astype(jnp.bfloat16)
    placed = jnp.dot(match.astype(jnp.bfloat16), doc_rows, preferred_element_type=jnp.float32)
    present = jnp.sum(match, axis=1, keepdims=True) > 0.5
    inputs = jnp.where(present, placed.astype(jnp.bfloat16), all_tokens)
    rows = jnp.concatenate([inputs, doc_rows], axis=0)
    logits = jnp.dot(rows, router_weight, preferred_element_type=jnp.float32)
    gates = gate_table(logits, jnp.concatenate([route_mask, doc_mask], axis=0))
    own_gates = lax.dynamic_slice_in_dim(gates, expert_base, local_count, 1).T[:, :, None]
    tok_count = halves * tok_rows
    doc_gates = gates[tok_count:]

    mixed_part, expert_grad, score_local = run_experts(
        rows,
        own_gates[:, :tok_count],
        own_gates[:, tok_count:],
        cotangent,
        w_gate,
        w_up,
        w_down,
    )
    given = lax.ppermute(mixed_part[tok_rows:].astype(jnp.bfloat16), "expert", swap)
    pair_sum = mixed_part[:tok_rows] + given.astype(jnp.float32)
    summed = lax.psum_scatter(pair_sum, "dp", scatter_dimension=0, tiled=True)
    mixed = summed.astype(jnp.bfloat16).reshape(1, out_rows, width)

    score_part = lax.dynamic_update_slice_in_dim(
        jnp.zeros((docs_count, EXPERTS), jnp.float32), score_local[:, :, 0].T, expert_base, 1
    )
    extra = jnp.zeros((count * LANES,), jnp.float32)
    extra = extra.at[: docs_count * EXPERTS].set(score_part.reshape(-1))
    packed = jnp.concatenate(
        [expert_grad.reshape(count, -1, LANES), extra.reshape(count, 1, LANES)], axis=1
    )
    both = sum_all(packed, 2)
    grad_sum = both[:, :-1].reshape(docs_count, width)
    scores = both[:, -1].reshape(-1)[: docs_count * EXPERTS].reshape(docs_count, EXPERTS)
    centre = jnp.sum(doc_gates * scores, axis=1, keepdims=True)
    router_grad = doc_gates * (scores - centre)
    grad_proj = grad_sum + jnp.dot(
        router_grad, router_weight.astype(jnp.float32).T, precision=PRECISE
    )
    grad_second = jnp.dot(activated.T, grad_proj, precision=PRECISE)
    grad_hidden = lax.dot_general(
        grad_proj, w_second, (((1,), (1,)), ((), ())), precision=PRECISE
    ) * gelu_slope(pre_act)
    grad_first = jnp.dot(grad_hidden.T, embed, precision=PRECISE)
    return (mixed, grad_first, grad_second)


def solution(mesh):
    placed = (
        P(("groups", "expert"), None),
        P(),
        P("expert", None, "dp"),
        P("expert", None, "dp"),
        P("expert", "dp", None),
        P(("groups", "expert"), None),
        P("groups"),
        P("groups", None),
        P(("dp", "expert"), None),
        P(("dp", "expert"), None),
        P("groups", None),
    )
    return jax.shard_map(
        body,
        mesh=mesh,
        in_specs=placed,
        out_specs=(
            P("expert", ("groups", "dp"), None),
            P(("groups", "dp", "expert"), None),
            P(("groups", "dp", "expert"), None),
        ),
        check_vma=False,
    )
```

time: 504 us -> 209 us (0.41)
  waiting for transfers between devices: 225 us -> 47.2 us
  matrix products: 143 us -> 20.2 us
  Pallas kernels: 0 us -> 108 us
  blocking collectives: 48.7 us -> 0 us
  local copies, waits for them, and re-layouts: 43.8 us -> 9.08 us
  other arithmetic: 23.9 us -> 8.84 us
    psum x2 -> x0, waiting for transfers between devices: 161 us -> none  [the longest x1 85.8 us: body(): lax.psum((jnp.dot(activated, w_second, precision=PRECISE), mask_part), ('...]
    dot_general x23 -> x4, matrix products: 127 us -> 4.9 us  [the longest x1 2.49 us: body(): jnp.dot(match.astype(jnp.bfloat16), doc_rows, preferred_element_type=jnp....]
    pallas_call x0 -> x3, Pallas kernels: none -> 108 us  [the longest x1 67.7 us: run_experts(): pl.pallas_call(functools.partial(expert_kernel, tok_count), grid=(local_c...]
    psum x1 -> x0, blocking collectives: 31.7 us -> none  [body(): lax.psum((jnp.dot(activated, w_second, precision=PRECISE), mask_part), ('...]
    gather x7 -> x0, local copies, waits for them, and re-layouts: 21.2 us -> none  [the longest x1 10.9 us: body(): picked = returned[target].reshape(tok_rows, TOP, width)]
    reduce_scatter x1, waiting for transfers between devices: 64.2 us -> 43.8 us  [body(): summed = lax.psum_scatter(pair_sum, 'dp', scatter_dimension=0, tiled=True)]
    all_to_all x2 -> x0, blocking collectives: 17 us -> none  [the longest x1 9.44 us: body(): lax.all_to_all(outgoing, 'expert', split_axis=0, concat_axis=0, tiled=True)]
    reduce_sum x2 -> x0, other arithmetic: 12.2 us -> none  [the longest x1 12.2 us: body(): partial_mixed = jnp.sum(chosen_gate[:, :, None] * picked, axis=1)]
  transfers between devices with their start and end apart: 3 -> 4, of which waited for: 3 -> 2; matrix products, arithmetic and copies ran while one was open for 6% -> 11% of each run, Pallas kernels for 0% -> 19%
where the time goes in v1:
time: 209 us
  Pallas kernels  108 us (52%)
  waiting for transfers between devices  47.2 us (23%)
  matrix products  20.2 us (10%)
  between operations  14.3 us (7%)
  local copies, waits for them, and re-layouts  9.08 us (4%)
  other arithmetic  8.84 us (4%)
    pallas_call x1, Pallas kernels, run_experts(): pl.pallas_call(functools.partial(expert_kernel, tok_count), grid=(local_c...  67.7 us
    reduce_scatter x1, waiting for transfers between devices, body(): summed = lax.psum_scatter(pair_sum, 'dp', scatter_dimension=0, tiled=True)  43.8 us
    pallas_call x2, Pallas kernels, sum_all(): pl.pallas_call(functools.partial(sum_kernel, dp_count, halves), out_shape...  40.5 us
    dot_general x1, matrix products, body(): grad_first = jnp.dot(grad_hidden.T, embed, precision=PRECISE)  4.31 us
    unnamed x28, local copies, waits for them, and re-layouts  4.22 us
  transfers between devices with their start and end apart: 4, of which 2 were waited for; matrix products, arithmetic and copies ran while one was open for 11% of the time, Pallas kernels for 19%

profile of v1, /device:TPU:0, one launch (start us, length us, event | category | flops | bytes accessed | tf_op | source)
XLA Modules:
  0.0 208.6 jit_solution(4246919641219515662)
XLA Ops:
  7.8 1.0 convert_reduce_fusion
  9.1 3.5 %fusion.26 = f32[16,192]{1,0:T(8,128)S(1)} fusion(f32[16,4096]{1,0:T(8,128)} %param.20, f32[192,4096]{1,0:T(8,128)S(1)} %copy-done), kind=kOutput, calls=%fused_computation.61 | convolution fusion | flops 150994944 | bytes 3420160 | tf_op jit(solution)/shard_map/dot_general | solution.py:224
  12.6 1.3 convolution_bitcast_fusion
  13.9 0.7 copy.29
  14.6 19.0 %shard_map.130 = f32[16,24,128]{2,1,0:T(8,128)} custom-call(f32[16,24,128]{2,1,0:T(8,128)} %bitcast.35), custom_call_target="tpu_custom_call" | custom-call | tf_op jit(solution)/shard_map/pallas_call | solution.py:91
  33.6 0.9 convert_element_type.28
  34.8 2.5 %maximum_select_fusion = bf16[512,3072]{1,0:T(8,128)(2,1)S(1)} fusion(bf16[256,3072]{1,0:T(8,128)(2,1)} %collective-permute-done, bf16[256,3072]{1,0:T(8,128)(2,1)S(1)} %copy-done.10, pred[512]{0:T(512)(128)(4,1)S(1)} %broadcast_compare_fusion, s32[512]{0:T(512)S(1)} %pad_add_fusion.1, s32[16]{0:T(128)S(1)} %copy-done.9, bf16[2,8,24,128]{3,2,1,0:T(8,128)(2,1)S(1)} %bitcast.37), kind=kOutput, calls=%fused_computation.4 | convolution fusion | flops 59793408 | bytes 6392384 | tf_op jit(solution)/shard_map/dot_general | solution.py:229
  38.1 1.0 multiply_reduce_fusion
  39.1 0.7 copy.27.doc_gates_ref
  39.8 1.0 copy.26.gates_ref
  40.8 67.7 %shard_map.131 = (f32[512,3072]{1,0:T(8,128)}, f32[16,3072]{1,0:T(8,128)}, f32[2,16,128]{2,1,0:T(8,128)}) custom-call(bf16[528,3072]{1,0:T(8,128)(2,1)} %copy-done.2, f32[2,512,1]{2,1,0:T(8,128)} %copy.26.gates_ref, f32[2,16,1]{2,1,0:T(8,128)} %copy.27.doc_gates_ref, bf16[16,3072]{1,0:T(8,128)(2,1)} %cot_ref.1, bf16[2,3072,2048]{2,1,0:T(8,128)(2,1)} %w_gate_ref.1, ...), custom_call_target="tpu_custom_call" | custom-call | tf_op jit(solution)/shard_map/pallas_call | solution.py:164
  108.5 2.1 %slice.66 = bf16[256,3072]{1,0:T(8,128)(2,1)S(1)} slice(f32[512,3072]{1,0:T(8,128)} %get-tuple-element.18), slice={[256:512], [0:3072]} | slice | bytes 3145728 | tf_op jit(solution)/shard_map/slice | solution.py:248
  110.8 3.3 %collective-permute-done.2 = bf16[256,3072]{1,0:T(8,128)(2,1)S(1)} collective-permute-done((bf16[256,3072]{1,0:T(8,128)(2,1)S(1)}, bf16[256,3072]{1,0:T(8,128)(2,1)S(1)}, u32[]{:S(2)}, u32[]{:S(2)}) %collective-permute-start.2) | collective-permute-done | bytes 1572896 | tf_op jit(solution)/shard_map/ppermute | solution.py:248
  114.1 4.1 %convert_add_fusion = f32[256,3072]{1,0:T(8,128)} fusion(bf16[256,3072]{1,0:T(8,128)(2,1)S(1)} %collective-permute-done.2, f32[512,3072]{1,0:T(8,128)} %get-tuple-element.18), kind=kLoop, calls=%fused_computation.5 | loop fusion | flops 1572864 | bytes 7864320 | tf_op jit(solution)/shard_map/add | solution.py:249
  118.3 0.9 copy-done.5
  119.9 0.7 pad_maximum_fusion.1.x_ref
  120.6 21.5 %shard_map.132 = f32[16,25,128]{2,1,0:T(8,128)} custom-call(f32[16,25,128]{2,1,0:T(8,128)} %pad_maximum_fusion.1.x_ref), custom_call_target="tpu_custom_call" | custom-call | tf_op jit(solution)/shard_map/pallas_call | solution.py:91
  142.2 1.0 slice.47
  143.2 0.9 slice_reduce_fusion.1
  144.7 3.5 %fusion.23 = f32[192,3072]{1,0:T(8,128)} fusion(f32[16,3072]{1,0:T(8,128)S(1)} %convolution_add_fusion, f32[16,192]{1,0:T(8,128)S(1)} %fusion.26), kind=kOutput, calls=%fused_computation.60 | convolution fusion | flops 113442816 | bytes 2568192 | tf_op jit(solution)/shard_map/dot_general | solution.py:269
  148.2 3.7 %convolution_multiply_fusion = f32[16,192]{1,0:T(8,128)S(1)} fusion(f32[16,3072]{1,0:T(8,128)S(1)} %convolution_add_fusion, f32[192,3072]{1,0:T(8,128)} %param.22, f32[16,192]{1,0:T(8,128)S(1)} %fusion.26), kind=kOutput, calls=%fused_computation.7 | convolution fusion | flops 113273856 | bytes 2580480 | tf_op jit(solution)/shard_map/dot_general | solution.py:270
  151.9 4.3 %fusion.27 = f32[192,4096]{1,0:T(8,128)} fusion(f32[16,192]{1,0:T(8,128)S(1)} %convolution_multiply_fusion, f32[16,4096]{1,0:T(8,128)S(1)} %copy-done.4), kind=kOutput, calls=%fused_computation.62 | convolution fusion | flops 150994944 | bytes 3420160 | tf_op jit(solution)/shard_map/dot_general | solution.py:273
  156.2 43.8 %reduce-scatter.2.cloned.1.call-done = f32[32,3072]{1,0:T(8,128)} async-done(((f32[256,3072]{1,0:T(8,128)}), f32[32,3072]{1,0:T(8,128)}) %reduce-scatter.2.cloned.1.call-update) | async-done | bytes 393232 | tf_op jit(solution)/shard_map/reduce_scatter | solution.py:250
  200.0 1.7 convert_bitcast_fusion
  (52 shorter events, 3.4 us)
Async XLA Ops:
  7.2 1.9 copy-start
  7.2 192.9 %reduce-scatter.2.cloned.1.call-start = ((), (), s32[]{:S(2)}) async-start(), calls=%async_computation.1 | async-start | bytes 3538944 | tf_op jit(solution)/shard_map/reduce_scatter | solution.py:250
  7.2 27.6 %collective-permute-start = (bf16[256,3072]{1,0:T(8,128)(2,1)}, bf16[256,3072]{1,0:T(8,128)(2,1)}, u32[]{:S(2)}, u32[]{:S(2)}) collective-permute-start(bf16[256,3072]{1,0:T(8,128)(2,1)} %param.13), channel_id=1, source_target_pairs={{0,1},{1,0},{2,3},{3,2},{4,5},{5,4},{6,7},{7,6},{8,9},{9,8},{10,11... | collective-permute-start | bytes 4718600 | tf_op jit(solution)/shard_map/ppermute | solution.py:214
  7.7 26.8 %collective-permute-start.1 = (s32[256,2]{0,1:T(2,128)}, s32[256,2]{0,1:T(2,128)S(1)}, u32[]{:S(2)}, u32[]{:S(2)}) collective-permute-start(s32[256,2]{0,1:T(2,128)} %param.18), channel_id=1, source_target_pairs={{0,1},{1,0},{2,3},{3,2},{4,5},{5,4},{6,7},{7,6},{8,9},{9,8},{10,11... | collective-permute-start | bytes 6152 | tf_op jit(solution)/shard_map/ppermute | solution.py:215
  7.8 4.8 %copy-start.3 = (f32[192,3072]{1,0:T(8,128)S(1)}, f32[192,3072]{1,0:T(8,128)}, u32[]{:S(2)}) copy-start(f32[192,3072]{1,0:T(8,128)} %param.22) | copy-start | bytes 7077892
  9.1 25.5 %copy-start.8 = (s32[256,2]{0,1:T(2,128)S(1)}, s32[256,2]{0,1:T(2,128)}, u32[]{:S(2)}) copy-start(s32[256,2]{0,1:T(2,128)} %param.18) | copy-start | bytes 6148
  9.1 25.5 %copy-start.9 = (s32[16]{0:T(128)S(1)}, s32[16]{0:T(128)}, u32[]{:S(2)}) copy-start(s32[16]{0:T(128)} %param.19) | copy-start | bytes 196
  12.6 22.2 %copy-start.10 = (bf16[256,3072]{1,0:T(8,128)(2,1)S(1)}, bf16[256,3072]{1,0:T(8,128)(2,1)}, u32[]{:S(2)}) copy-start(bf16[256,3072]{1,0:T(8,128)(2,1)} %param.13) | copy-start | bytes 4718596
  37.3 0.7 copy-start.6
  38.1 2.8 %copy-start.2 = (bf16[528,3072]{1,0:T(8,128)(2,1)}, bf16[528,3072]{1,0:T(8,128)(2,1)S(1)}, u32[]{:S(2)}) copy-start(bf16[528,3072]{1,0:T(8,128)(2,1)S(1)} %pad_maximum_fusion.rows_ref) | copy-start | bytes 9732100
  110.6 3.5 %collective-permute-start.2 = (bf16[256,3072]{1,0:T(8,128)(2,1)S(1)}, bf16[256,3072]{1,0:T(8,128)(2,1)S(1)}, u32[]{:S(2)}, u32[]{:S(2)}) collective-permute-start(bf16[256,3072]{1,0:T(8,128)(2,1)S(1)} %slice.66), channel_id=1, source_target_pairs={{0,1},{1,0},{2,3},{3,2},{4,5},{5,4},{6,7},{7,6},{8,9},{9,8},{10,11... | collective-permute-start | bytes 4718600 | tf_op jit(solution)/shard_map/ppermute | solution.py:248
  118.2 0.9 copy-start.5
  118.3 1.0 copy-start.7
  142.2 9.8 %copy-start.4 = (f32[16,4096]{1,0:T(8,128)S(1)}, f32[16,4096]{1,0:T(8,128)}, u32[]{:S(2)}) copy-start(f32[16,4096]{1,0:T(8,128)} %param.20) | copy-start | bytes 786436
  144.7 57.0 %copy-start.1 = (f32[192,4096]{1,0:T(8,128)S(1)}, f32[192,4096]{1,0:T(8,128)}, u32[]{:S(2)}) copy-start(f32[192,4096]{1,0:T(8,128)} %param.21) | copy-start | bytes 9437188
Sparse Core Ops, SparseCore 0:
  118.4 81.6 reduce-scatter.1

commit v2 on v1

--- a/solution.py
+++ b/solution.py
@@ -104,6 +104,166 @@
     )(x)
 
 
+def finish_kernel(
+    dp_count,
+    halves,
+    x_ref,
+    part_ref,
+    out_ref,
+    mixed_ref,
+    land,
+    total,
+    pair_land,
+    near_send,
+    near_land,
+    far_send,
+    far_land,
+    sems,
+    pair_sems,
+    near_sems,
+    far_sems,
+):
+    count = dp_count * halves
+    groups = dp_count // 2
+    dp = lax.axis_index("dp")
+    half = lax.axis_index("expert")
+    me = dp * halves + half
+    high, low = dp // 2, lax.rem(dp, 2)
+
+    def place(step):
+        other = lax.rem(me + step, count)
+        return other, {"dp": other // halves, "expert": lax.rem(other, halves)}
+
+    barrier = pltpu.get_barrier_semaphore()
+    for step in range(1, count):
+        pl.semaphore_signal(
+            barrier, inc=1, device_id=place(step)[1], device_id_type=pl.DeviceIdType.MESH
+        )
+    pl.semaphore_wait(barrier, count - 1)
+
+    def copy(source, target, table, row, step, device):
+        return pltpu.make_async_remote_copy(
+            src_ref=source,
+            dst_ref=target,
+            send_sem=table.at[row, step],
+            recv_sem=table.at[row + 1, step],
+            device_id=device,
+            device_id_type=pl.DeviceIdType.MESH,
+        )
+
+    def scatter(step):
+        other, device = place(step)
+        return copy(x_ref.at[other], land.at[step], sems, 0, step, device)
+
+    def spread(step):
+        return copy(total.at[me], total.at[me], sems, 2, step, place(step)[1])
+
+    def goal(step, side):
+        return 2 * lax.rem(high + 1 + step, groups) + side
+
+    def pair(step, away):
+        index = goal(step, (1 - low) if away else low)
+        slot = step + (0 if away else groups)
+        return copy(
+            part_ref.at[1, index],
+            pair_land.at[slot],
+            pair_sems,
+            0,
+            slot,
+            {"expert": 1 - half},
+        )
+
+    def near(step):
+        return copy(
+            near_send.at[step], near_land.at[step], near_sems, 0, step, {"dp": 2 * high + 1 - low}
+        )
+
+    def far(step):
+        return copy(
+            far_send.at[step], far_land.at[step], far_sems, 0, step, {"dp": goal(step, low)}
+        )
+
+    for step in range(1, count):
+        scatter(step).start()
+    for step in range(groups):
+        pair(step, True).start()
+    for step in range(groups):
+        pair(step, False).start()
+    for step in range(groups):
+        pair(step, True).wait_recv()
+        near_send[step] = (
+            part_ref[0, goal(step, 1 - low)].astype(jnp.float32)
+            + pair_land[step].astype(jnp.float32)
+        ).astype(jnp.bfloat16)
+        near(step).start()
+    acc = x_ref[me]
+    for step in range(1, count):
+        scatter(step).wait_recv()
+        acc = acc + land[step]
+    total[me] = acc
+    for step in range(1, count):
+        spread(step).start()
+    for step in range(groups):
+        pair(step, False).wait_recv()
+        near(step).wait_recv()
+        block = (
+            part_ref[0, goal(step, low)].astype(jnp.float32)
+            + pair_land[groups + step].astype(jnp.float32)
+            + near_land[step].astype(jnp.float32)
+        )
+        if step < groups - 1:
+            far_send[step] = block.astype(jnp.bfloat16)
+            far(step).start()
+    for step in range(groups - 1):
+        far(step).wait_recv()
+        block = block + far_land[step].astype(jnp.float32)
+    mixed_ref[...] = block.astype(jnp.bfloat16)
+    for step in range(1, count):
+        scatter(step).wait_send()
+        spread(step).wait()
+    out_ref[...] = total[...]
+    for step in range(groups):
+        pair(step, True).wait_send()
+        pair(step, False).wait_send()
+        near(step).wait_send()
+    for step in range(groups - 1):
+        far(step).wait_send()
+
+
+def finish(x, part, collective_id):
+    dp_count = lax.axis_size("dp")
+    halves = lax.axis_size("expert")
+    count = dp_count * halves
+    groups = dp_count // 2
+    block = part.shape[2:]
+    whole = pl.BlockSpec(memory_space=pltpu.VMEM)
+    return pl.pallas_call(
+        functools.partial(finish_kernel, dp_count, halves),
+        out_shape=(
+            jax.ShapeDtypeStruct(x.shape, x.dtype),
+            jax.ShapeDtypeStruct(block, jnp.bfloat16),
+        ),
+        in_specs=[whole, whole],
+        out_specs=(whole, whole),
+        scratch_shapes=[
+            pltpu.VMEM(x.shape, x.dtype),
+            pltpu.VMEM(x.shape, x.dtype),
+            pltpu.VMEM((dp_count,) + block, jnp.bfloat16),
+            pltpu.VMEM((groups,) + block, jnp.bfloat16),
+            pltpu.VMEM((groups,) + block, jnp.bfloat16),
+            pltpu.VMEM((groups,) + block, jnp.bfloat16),
+            pltpu.VMEM((groups,) + block, jnp.bfloat16),
+            pltpu.SemaphoreType.DMA((4, count)),
+            pltpu.SemaphoreType.DMA((2, dp_count)),
+            pltpu.SemaphoreType.DMA((2, groups)),
+            pltpu.SemaphoreType.DMA((2, groups)),
+        ],
+        compiler_params=pltpu.CompilerParams(
+            collective_id=collective_id, has_side_effects=True, vmem_limit_bytes=VMEM_BYTES
+        ),
+    )(x, part)
+
+
 def expert_kernel(
     tok_count,
     rows_ref,
@@ -116,12 +276,13 @@
     mixed_ref,
     grad_ref,
     score_ref,
+    total,
 ):
     first = (pl.program_id(0) == 0) & (pl.program_id(1) == 0)
 
     @pl.when(first)
     def _():
-        mixed_ref[...] = jnp.zeros_like(mixed_ref)
+        total[...] = jnp.zeros_like(total)
         grad_ref[...] = jnp.zeros_like(grad_ref)
 
     @pl.when(pl.program_id(1) == 0)
@@ -138,7 +299,7 @@
     silu = gate_pre * sigma
     product = silu * up_pre
     hidden = (product[:tok_count] * gates_ref[0]).astype(jnp.bfloat16)
-    mixed_ref[...] += jnp.dot(hidden, w_down, preferred_element_type=jnp.float32)
+    total[...] += jnp.dot(hidden, w_down, preferred_element_type=jnp.float32)
     doc_gate = gate_pre[tok_count:]
     doc_up = up_pre[tok_count:]
     doc_sigma = sigma[tok_count:]
@@ -153,6 +314,14 @@
     gate_grad = (scaled * doc_up * slope).astype(jnp.bfloat16)
     grad_ref[...] += contract_last(gate_grad, w_gate) + contract_last(up_grad, w_up)
 
+    last = (pl.program_id(0) == pl.num_programs(0) - 1) & (
+        pl.program_id(1) == pl.num_programs(1) - 1
+    )
+
+    @pl.when(last)
+    def _():
+        mixed_ref[...] = total[...].astype(jnp.bfloat16)
+
 
 def run_experts(rows, gates, doc_gates, cotangent, w_gate, w_up, w_down):
     local_count, width, ff = w_gate.shape
@@ -165,7 +334,7 @@
         functools.partial(expert_kernel, tok_count),
         grid=(local_count, ff // tile),
         out_shape=(
-            jax.ShapeDtypeStruct((tok_count, width), jnp.float32),
+            jax.ShapeDtypeStruct((tok_count, width), jnp.bfloat16),
             jax.ShapeDtypeStruct((docs_count, width), jnp.float32),
             jax.ShapeDtypeStruct((local_count, docs_count, LANES), jnp.float32),
         ),
@@ -183,6 +352,7 @@
             pl.BlockSpec((docs_count, width), fixed),
             pl.BlockSpec((1, docs_count, LANES), of_expert),
         ),
+        scratch_shapes=[pltpu.VMEM((tok_count, width), jnp.float32)],
         compiler_params=pltpu.CompilerParams(vmem_limit_bytes=VMEM_BYTES),
     )(rows, gates, doc_gates, cotangent, w_gate, w_up, w_down)
 
@@ -245,11 +415,6 @@
         w_up,
         w_down,
     )
-    given = lax.ppermute(mixed_part[tok_rows:].astype(jnp.bfloat16), "expert", swap)
-    pair_sum = mixed_part[:tok_rows] + given.astype(jnp.float32)
-    summed = lax.psum_scatter(pair_sum, "dp", scatter_dimension=0, tiled=True)
-    mixed = summed.astype(jnp.bfloat16).reshape(1, out_rows, width)
-
     score_part = lax.dynamic_update_slice_in_dim(
         jnp.zeros((docs_count, EXPERTS), jnp.float32), score_local[:, :, 0].T, expert_base, 1
     )
@@ -258,7 +423,10 @@
     packed = jnp.concatenate(
         [expert_grad.reshape(count, -1, LANES), extra.reshape(count, 1, LANES)], axis=1
     )
-    both = sum_all(packed, 2)
+    both, scattered = finish(
+        packed, mixed_part.reshape(halves, dp_count, out_rows, width), 2
+    )
+    mixed = scattered.reshape(1, out_rows, width)
     grad_sum = both[:, :-1].reshape(docs_count, width)
     scores = both[:, -1].reshape(-1)[: docs_count * EXPERTS].reshape(docs_count, EXPERTS)
     centre = jnp.sum(doc_gates * scores, axis=1, keepdims=True)

time: 209 us -> 158 us (0.76)
  waiting for transfers between devices: 47.2 us -> 0.01 us
  Pallas kernels: 108 us -> 124 us
  between operations: 14.3 us -> 0.88 us
  other arithmetic: 8.84 us -> 3.01 us
    reduce_scatter x1 -> x0, waiting for transfers between devices: 43.8 us -> none  [body(): summed = lax.psum_scatter(pair_sum, 'dp', scatter_dimension=0, tiled=True)]
    pallas_call x0 -> x1, Pallas kernels: none -> 36.2 us  [finish(): pl.pallas_call(functools.partial(finish_kernel, dp_count, halves), out_sh...]
    pallas_call x2 -> x1, Pallas kernels: 40.5 us -> 19 us  [sum_all(): pl.pallas_call(functools.partial(sum_kernel, dp_count, halves), out_shape...]
    add x1 -> x0, other arithmetic: 4.14 us -> none  [body(): pair_sum = mixed_part[:tok_rows] + given.astype(jnp.float32)]
    ppermute x1 -> x0, waiting for transfers between devices: 3.33 us -> none  [body(): lax.ppermute(mixed_part[tok_rows:].astype(jnp.bfloat16), 'expert', swap)]
    slice x1 -> x0, local copies, waits for them, and re-layouts: 2.1 us -> none  [body(): mixed_part[tok_rows:].astype(jnp.bfloat16)]
    unnamed x28 -> x27, local copies, waits for them, and re-layouts: 4.22 us -> 4.97 us
  transfers between devices with their start and end apart: 4 -> 2, of which waited for: 2 -> 0; matrix products, arithmetic and copies ran while one was open for 11% -> 5% of each run, Pallas kernels for 19% -> 12%
where the time goes in v2:
time: 158 us; the launch traced here: 157 us
  Pallas kernels  124 us (78%)
  matrix products  20.2 us (13%)
  local copies, waits for them, and re-layouts  8.45 us (5%)
  other arithmetic  3.01 us (2%)
    pallas_call x1, Pallas kernels, run_experts(): pl.pallas_call(functools.partial(expert_kernel, tok_count), grid=(local_c...  69 us
    pallas_call x1, Pallas kernels, finish(): pl.pallas_call(functools.partial(finish_kernel, dp_count, halves), out_sh...  36.2 us
    pallas_call x1, Pallas kernels, sum_all(): pl.pallas_call(functools.partial(sum_kernel, dp_count, halves), out_shape...  19 us
    unnamed x27, local copies, waits for them, and re-layouts  4.97 us
    dot_general x1, matrix products, body(): grad_first = jnp.dot(grad_hidden.T, embed, precision=PRECISE)  4.31 us
    dot_general x1, matrix products, body(): lax.dot_general(grad_proj, w_second, (((1,), (1,)), ((), ())), precision=...  3.75 us
    dot_general x1, matrix products, body(): lax.dot_general(embed, w_first, (((1,), (1,)), ((), ())), precision=PRECISE)  3.51 us
    dot_general x1, matrix products, body(): grad_second = jnp.dot(activated.T, grad_proj, precision=PRECISE)  3.47 us
  transfers between devices with their start and end apart: 2, of which 0 were waited for; matrix products, arithmetic and copies ran while one was open for 5% of the time, Pallas kernels for 12%

profile of v2, /device:TPU:0, one launch (start us, length us, event | category | flops | bytes accessed | tf_op | source)
XLA Modules:
  0.0 157.5 jit_solution(14480125278059652458)
XLA Ops:
  0.6 0.5 collective-permute-start
  1.3 1.0 convert_reduce_fusion
  2.5 3.5 %fusion.26 = f32[16,192]{1,0:T(8,128)S(1)} fusion(f32[16,4096]{1,0:T(8,128)} %param.20, f32[192,4096]{1,0:T(8,128)S(1)} %copy-done), kind=kOutput, calls=%fused_computation.58 | convolution fusion | flops 150994944 | bytes 3420160 | tf_op jit(solution)/shard_map/dot_general | solution.py:394
  6.1 1.3 convolution_bitcast_fusion
  7.3 0.7 copy.29
  8.1 19.0 %shard_map.130 = f32[16,24,128]{2,1,0:T(8,128)} custom-call(f32[16,24,128]{2,1,0:T(8,128)} %bitcast.36), custom_call_target="tpu_custom_call" | custom-call | tf_op jit(solution)/shard_map/pallas_call | solution.py:91
  27.1 0.9 convert_element_type.21
  28.3 2.5 %maximum_select_fusion = bf16[512,3072]{1,0:T(8,128)(2,1)S(1)} fusion(bf16[256,3072]{1,0:T(8,128)(2,1)} %collective-permute-done, bf16[256,3072]{1,0:T(8,128)(2,1)S(1)} %copy-done.9, pred[512]{0:T(512)(128)(4,1)S(1)} %broadcast_compare_fusion, s32[512]{0:T(512)S(1)} %pad_add_fusion.1, s32[16]{0:T(128)S(1)} %copy-done.8, bf16[2,8,24,128]{3,2,1,0:T(8,128)(2,1)S(1)} %bitcast.38), kind=kOutput, calls=%fused_computation.3 | convolution fusion | flops 59793408 | bytes 6392384 | tf_op jit(solution)/shard_map/dot_general | solution.py:399
  31.0 0.5 copy-done.6
  31.6 1.0 multiply_reduce_fusion
  32.6 1.0 copy.26.gates_ref
  33.6 0.7 copy.27.doc_gates_ref
  34.3 69.0 %shard_map.131 = (bf16[512,3072]{1,0:T(8,128)(2,1)}, f32[16,3072]{1,0:T(8,128)}, f32[2,16,128]{2,1,0:T(8,128)}) custom-call(bf16[528,3072]{1,0:T(8,128)(2,1)} %copy-done.2, f32[2,512,1]{2,1,0:T(8,128)} %copy.26.gates_ref, f32[2,16,1]{2,1,0:T(8,128)} %copy.27.doc_gates_ref, bf16[16,3072]{1,0:T(8,128)(2,1)} %cot_ref.1, bf16[2,3072,2048]{2,1,0:T(8,128)(2,1)} %w_gate_ref.1, ...), custom_call_target="tpu_custom_call" | custom-call | tf_op jit(solution)/shard_map/pallas_call | solution.py:333
  103.3 1.0 copy.31
  104.3 0.8 slice_reduce_fusion
  105.2 0.4 dynamic_update_slice.3
  105.7 0.7 pad_maximum_fusion.1.x_ref
  106.4 36.2 %shard_map.132 = (f32[16,25,128]{2,1,0:T(8,128)}, bf16[32,3072]{1,0:T(8,128)(2,1)}) custom-call(f32[16,25,128]{2,1,0:T(8,128)} %pad_maximum_fusion.1.x_ref, bf16[2,8,32,3072]{3,2,1,0:T(8,128)(2,1)} %bitcast.33), custom_call_target="tpu_custom_call" | custom-call | tf_op jit(solution)/shard_map/pallas_call | solution.py:240
  142.7 0.9 slice_reduce_fusion.1
  143.6 0.9 slice.38
  145.2 3.8 %convolution_multiply_fusion = f32[16,192]{1,0:T(8,128)S(1)} fusion(f32[16,3072]{1,0:T(8,128)S(1)} %convolution_add_fusion, f32[192,3072]{1,0:T(8,128)} %param.22, f32[16,192]{1,0:T(8,128)S(1)} %fusion.26), kind=kOutput, calls=%fused_computation.5 | convolution fusion | flops 113273856 | bytes 2580480 | tf_op jit(solution)/shard_map/dot_general | solution.py:438
  149.0 3.5 %fusion.23 = f32[192,3072]{1,0:T(8,128)} fusion(f32[16,3072]{1,0:T(8,128)S(1)} %convolution_add_fusion, f32[16,192]{1,0:T(8,128)S(1)} %fusion.26), kind=kOutput, calls=%fused_computation.57 | convolution fusion | flops 113442816 | bytes 2568192 | tf_op jit(solution)/shard_map/dot_general | solution.py:437
  152.5 4.3 %fusion.27 = f32[192,4096]{1,0:T(8,128)} fusion(f32[16,192]{1,0:T(8,128)S(1)} %convolution_multiply_fusion, f32[16,4096]{1,0:T(8,128)S(1)} %copy-done.4), kind=kOutput, calls=%fused_computation.59 | convolution fusion | flops 150994944 | bytes 3420160 | tf_op jit(solution)/shard_map/dot_general | solution.py:441
  156.8 0.7 copy.39
  (43 shorter events, 1.7 us)
Async XLA Ops:
  0.6 1.9 %copy-start = (f32[192,4096]{1,0:T(8,128)S(1)}, f32[192,4096]{1,0:T(8,128)}, u32[]{:S(2)}) copy-start(f32[192,4096]{1,0:T(8,128)} %param.21) | copy-start | bytes 9437188
  0.6 27.6 %collective-permute-start = (bf16[256,3072]{1,0:T(8,128)(2,1)}, bf16[256,3072]{1,0:T(8,128)(2,1)}, u32[]{:S(2)}, u32[]{:S(2)}) collective-permute-start(bf16[256,3072]{1,0:T(8,128)(2,1)} %param.13), channel_id=1, source_target_pairs={{0,1},{1,0},{2,3},{3,2},{4,5},{5,4},{6,7},{7,6},{8,9},{9,8},{10,11... | collective-permute-start | bytes 4718600 | tf_op jit(solution)/shard_map/ppermute | solution.py:384
  1.2 26.9 %collective-permute-start.1 = (s32[256,2]{0,1:T(2,128)}, s32[256,2]{0,1:T(2,128)S(1)}, u32[]{:S(2)}, u32[]{:S(2)}) collective-permute-start(s32[256,2]{0,1:T(2,128)} %param.18), channel_id=1, source_target_pairs={{0,1},{1,0},{2,3},{3,2},{4,5},{5,4},{6,7},{7,6},{8,9},{9,8},{10,11... | collective-permute-start | bytes 6152 | tf_op jit(solution)/shard_map/ppermute | solution.py:385
  1.2 4.8 %copy-start.3 = (f32[192,3072]{1,0:T(8,128)S(1)}, f32[192,3072]{1,0:T(8,128)}, u32[]{:S(2)}) copy-start(f32[192,3072]{1,0:T(8,128)} %param.22) | copy-start | bytes 7077892
  2.5 25.5 %copy-start.7 = (s32[256,2]{0,1:T(2,128)S(1)}, s32[256,2]{0,1:T(2,128)}, u32[]{:S(2)}) copy-start(s32[256,2]{0,1:T(2,128)} %param.18) | copy-start | bytes 6148
  2.5 25.5 %copy-start.8 = (s32[16]{0:T(128)S(1)}, s32[16]{0:T(128)}, u32[]{:S(2)}) copy-start(s32[16]{0:T(128)} %param.19) | copy-start | bytes 196
  6.1 22.2 %copy-start.9 = (bf16[256,3072]{1,0:T(8,128)(2,1)S(1)}, bf16[256,3072]{1,0:T(8,128)(2,1)}, u32[]{:S(2)}) copy-start(bf16[256,3072]{1,0:T(8,128)(2,1)} %param.13) | copy-start | bytes 4718596
  30.8 0.7 copy-start.6
  31.6 2.7 %copy-start.2 = (bf16[528,3072]{1,0:T(8,128)(2,1)}, bf16[528,3072]{1,0:T(8,128)(2,1)S(1)}, u32[]{:S(2)}) copy-start(bf16[528,3072]{1,0:T(8,128)(2,1)S(1)} %pad_maximum_fusion.rows_ref) | copy-start | bytes 9732100
  142.7 9.8 %copy-start.4 = (f32[16,4096]{1,0:T(8,128)S(1)}, f32[16,4096]{1,0:T(8,128)}, u32[]{:S(2)}) copy-start(f32[16,4096]{1,0:T(8,128)} %param.20) | copy-start | bytes 786436
  145.2 12.2 %copy-start.1 = (f32[192,4096]{1,0:T(8,128)S(1)}, f32[192,4096]{1,0:T(8,128)}, u32[]{:S(2)}) copy-start(f32[192,4096]{1,0:T(8,128)} %param.21) | copy-start | bytes 9437188
  149.0 7.8 %copy-start.5 = (bf16[32,3072]{1,0:T(8,128)(2,1)S(1)}, bf16[32,3072]{1,0:T(8,128)(2,1)}, u32[]{:S(2)}) copy-start(bf16[32,3072]{1,0:T(8,128)(2,1)} %get-tuple-element.23) | copy-start | bytes 589828

commit v3 on v2

--- a/solution.py
+++ b/solution.py
@@ -31,72 +31,103 @@
     )
 
 
-def sum_kernel(dp_count, halves, x_ref, out_ref, land, total, sems):
-    count = dp_count * halves
-    me = lax.axis_index("dp") * halves + lax.axis_index("expert")
-
-    def place(step):
-        other = lax.rem(me + step, count)
-        return other, {"dp": other // halves, "expert": lax.rem(other, halves)}
+def sum_kernel(groups, x_ref, out_ref, near_land, part, far_land, total, near_sems, far_sems):
+    dp = lax.axis_index("dp")
+    half = lax.axis_index("expert")
+    high = dp // 2
+    low = lax.rem(dp, 2)
+    own = low * 2 + half
+
+    def near_place(step):
+        other = lax.rem(own + step, 4)
+        return other, {"dp": high * 2 + other // 2, "expert": lax.rem(other, 2)}
+
+    def far_place(step):
+        other = lax.rem(high + step, groups)
+        return other, {"dp": other * 2 + low}
 
     barrier = pltpu.get_barrier_semaphore()
-    for step in range(1, count):
+    for step in range(1, 4):
         pl.semaphore_signal(
-            barrier, inc=1, device_id=place(step)[1], device_id_type=pl.DeviceIdType.MESH
-        )
-    pl.semaphore_wait(barrier, count - 1)
-
-    def scatter(step):
-        other, device = place(step)
+            barrier, inc=1, device_id=near_place(step)[1], device_id_type=pl.DeviceIdType.MESH
+        )
+    for step in range(1, groups):
+        pl.semaphore_signal(
+            barrier, inc=1, device_id=far_place(step)[1], device_id_type=pl.DeviceIdType.MESH
+        )
+    pl.semaphore_wait(barrier, 3 + groups - 1)
+
+    def copy(source, target, table, row, step, device):
         return pltpu.make_async_remote_copy(
-            src_ref=x_ref.at[other],
-            dst_ref=land.at[step],
-            send_sem=sems.at[0, step],
-            recv_sem=sems.at[1, step],
+            src_ref=source,
+            dst_ref=target,
+            send_sem=table.at[row, step],
+            recv_sem=table.at[row + 1, step],
             device_id=device,
             device_id_type=pl.DeviceIdType.MESH,
         )
 
-    def spread(step):
-        return pltpu.make_async_remote_copy(
-            src_ref=total.at[me],
-            dst_ref=total.at[me],
-            send_sem=sems.at[2, step],
-            recv_sem=sems.at[3, step],
-            device_id=place(step)[1],
-            device_id_type=pl.DeviceIdType.MESH,
-        )
-
-    for step in range(1, count):
-        scatter(step).start()
-    acc = x_ref[me]
-    for step in range(1, count):
-        scatter(step).wait_recv()
-        acc = acc + land[step]
-    total[me] = acc
-    for step in range(1, count):
-        spread(step).start()
-    for step in range(1, count):
-        scatter(step).wait_send()
-    for step in range(1, count):
-        spread(step).wait()
+    def near_scatter(step):
+        other, device = near_place(step)
+        return copy(x_ref.at[other], near_land.at[step], near_sems, 0, step, device)
+
+    def far_scatter(step):
+        other, device = far_place(step)
+        return copy(part.at[other], far_land.at[step], far_sems, 0, step, device)
+
+    def far_spread(step):
+        piece = total.at[own, high]
+        return copy(piece, piece, far_sems, 2, step, far_place(step)[1])
+
+    def near_spread(step):
+        piece = total.at[own]
+        return copy(piece, piece, near_sems, 2, step, near_place(step)[1])
+
+    for step in range(1, 4):
+        near_scatter(step).start()
+    acc = x_ref[own]
+    for step in range(1, 4):
+        near_scatter(step).wait_recv()
+        acc = acc + near_land[step]
+    part[...] = acc
+    for step in range(1, groups):
+        far_scatter(step).start()
+    piece = part[high]
+    for step in range(1, groups):
+        far_scatter(step).wait_recv()
+        piece = piece + far_land[step]
+    total[own, high] = piece
+    for step in range(1, groups):
+        far_spread(step).start()
+    for step in range(1, groups):
+        far_spread(step).wait_recv()
+    for step in range(1, 4):
+        near_spread(step).start()
+    for step in range(1, 4):
+        near_scatter(step).wait_send()
+    for step in range(1, groups):
+        far_scatter(step).wait_send()
+        far_spread(step).wait_send()
+    for step in range(1, 4):
+        near_spread(step).wait()
     out_ref[...] = total[...]
 
 
 def sum_all(x, collective_id):
-    dp_count = lax.axis_size("dp")
-    halves = lax.axis_size("expert")
-    count = dp_count * halves
-    rows = x.shape[1]
+    groups = lax.axis_size("dp") // 2
+    x = x.reshape((4, groups) + x.shape[1:])
     return pl.pallas_call(
-        functools.partial(sum_kernel, dp_count, halves),
+        functools.partial(sum_kernel, groups),
         out_shape=jax.ShapeDtypeStruct(x.shape, x.dtype),
         in_specs=[pl.BlockSpec(memory_space=pltpu.VMEM)],
         out_specs=pl.BlockSpec(memory_space=pltpu.VMEM),
         scratch_shapes=[
-            pltpu.VMEM((count, rows, LANES), x.dtype),
-            pltpu.VMEM((count, rows, LANES), x.dtype),
-            pltpu.SemaphoreType.DMA((4, count)),
+            pltpu.VMEM(x.shape, x.dtype),
+            pltpu.VMEM(x.shape[1:], x.dtype),
+            pltpu.VMEM(x.shape[1:], x.dtype),
+            pltpu.VMEM(x.shape, x.dtype),
+            pltpu.SemaphoreType.DMA((4, 4)),
+            pltpu.SemaphoreType.DMA((4, groups)),
         ],
         compiler_params=pltpu.CompilerParams(
             collective_id=collective_id, has_side_effects=True

time: 158 us -> 157 us (level)
    pallas_call x1, Pallas kernels: 36.2 us -> 34.4 us  [finish(): pl.pallas_call(functools.partial(finish_kernel, dp_count, halves), out_sh...]
    pallas_call x1, Pallas kernels: 19 us -> 20.6 us  [sum_all(): pl.pallas_call(functools.partial(sum_kernel, groups), out_shape=jax.Shape...]
  transfers between devices with their start and end apart: 2 -> 2, of which waited for: 0 -> 0; matrix products, arithmetic and copies ran while one was open for 5% -> 5% of each run, Pallas kernels for 12% -> 13%
where the time goes in v3:
time: 157 us
  Pallas kernels  124 us (79%)
  matrix products  20.3 us (13%)
  local copies, waits for them, and re-layouts  8.41 us (5%)
  other arithmetic  3.01 us (2%)
    pallas_call x1, Pallas kernels, run_experts(): pl.pallas_call(functools.partial(expert_kernel, tok_count), grid=(local_c...  68.9 us
    pallas_call x1, Pallas kernels, finish(): pl.pallas_call(functools.partial(finish_kernel, dp_count, halves), out_sh...  34.4 us
    pallas_call x1, Pallas kernels, sum_all(): pl.pallas_call(functools.partial(sum_kernel, groups), out_shape=jax.Shape...  20.6 us
    unnamed x27, local copies, waits for them, and re-layouts  4.97 us
    dot_general x1, matrix products, body(): grad_first = jnp.dot(grad_hidden.T, embed, precision=PRECISE)  4.31 us
    dot_general x1, matrix products, body(): lax.dot_general(grad_proj, w_second, (((1,), (1,)), ((), ())), precision=...  3.75 us
    dot_general x1, matrix products, body(): lax.dot_general(embed, w_first, (((1,), (1,)), ((), ())), precision=PRECISE)  3.51 us
    dot_general x1, matrix products, body(): grad_second = jnp.dot(activated.T, grad_proj, precision=PRECISE)  3.47 us
  transfers between devices with their start and end apart: 2, of which 0 were waited for; matrix products, arithmetic and copies ran while one was open for 5% of the time, Pallas kernels for 13%

profile of v3, /device:TPU:0, one launch (start us, length us, event | category | flops | bytes accessed | tf_op | source)
XLA Modules:
  0.0 157.0 jit_solution(13946089529016169877)
XLA Ops:
  0.6 0.5 collective-permute-start
  1.3 1.0 convert_reduce_fusion
  2.5 3.5 %fusion.26 = f32[16,192]{1,0:T(8,128)S(1)} fusion(f32[16,4096]{1,0:T(8,128)} %param.20, f32[192,4096]{1,0:T(8,128)S(1)} %copy-done), kind=kOutput, calls=%fused_computation.58 | convolution fusion | flops 150994944 | bytes 3420160 | tf_op jit(solution)/shard_map/dot_general | solution.py:425
  6.1 1.3 convolution_bitcast_fusion
  7.3 0.7 copy.29
  8.1 20.6 %shard_map.130 = f32[4,4,24,128]{3,2,1,0:T(8,128)} custom-call(f32[4,4,24,128]{3,2,1,0:T(8,128)} %bitcast.38), custom_call_target="tpu_custom_call" | custom-call | tf_op jit(solution)/shard_map/pallas_call | solution.py:119
  28.7 0.9 convert_element_type.21
  29.9 2.5 %maximum_select_fusion = bf16[512,3072]{1,0:T(8,128)(2,1)S(1)} fusion(bf16[256,3072]{1,0:T(8,128)(2,1)} %collective-permute-done, bf16[256,3072]{1,0:T(8,128)(2,1)S(1)} %copy-done.9, pred[512]{0:T(512)(128)(4,1)S(1)} %broadcast_compare_fusion, s32[512]{0:T(512)S(1)} %pad_add_fusion.1, s32[16]{0:T(128)S(1)} %copy-done.8, bf16[2,8,24,128]{3,2,1,0:T(8,128)(2,1)S(1)} %bitcast.40), kind=kOutput, calls=%fused_computation.3 | convolution fusion | flops 59793408 | bytes 6392384 | tf_op jit(solution)/shard_map/dot_general | solution.py:430
  32.6 0.5 copy-done.6
  33.1 1.0 multiply_reduce_fusion
  34.2 1.0 copy.26.gates_ref
  35.2 0.7 copy.27.doc_gates_ref
  35.9 68.9 %shard_map.131 = (bf16[512,3072]{1,0:T(8,128)(2,1)}, f32[16,3072]{1,0:T(8,128)}, f32[2,16,128]{2,1,0:T(8,128)}) custom-call(bf16[528,3072]{1,0:T(8,128)(2,1)} %copy-done.2, f32[2,512,1]{2,1,0:T(8,128)} %copy.26.gates_ref, f32[2,16,1]{2,1,0:T(8,128)} %copy.27.doc_gates_ref, bf16[16,3072]{1,0:T(8,128)(2,1)} %cot_ref.1, bf16[2,3072,2048]{2,1,0:T(8,128)(2,1)} %w_gate_ref.1, ...), custom_call_target="tpu_custom_call" | custom-call | tf_op jit(solution)/shard_map/pallas_call | solution.py:364
  104.8 1.0 copy.31
  105.7 0.8 slice_reduce_fusion
  106.6 0.3 dynamic_update_slice.3
  107.1 0.7 pad_maximum_fusion.1.x_ref
  107.8 34.4 %shard_map.132 = (f32[16,25,128]{2,1,0:T(8,128)}, bf16[32,3072]{1,0:T(8,128)(2,1)}) custom-call(f32[16,25,128]{2,1,0:T(8,128)} %pad_maximum_fusion.1.x_ref, bf16[2,8,32,3072]{3,2,1,0:T(8,128)(2,1)} %bitcast.35), custom_call_target="tpu_custom_call" | custom-call | tf_op jit(solution)/shard_map/pallas_call | solution.py:271
  142.2 0.9 slice_reduce_fusion.1
  143.1 0.9 slice.38
  144.8 3.8 %convolution_multiply_fusion = f32[16,192]{1,0:T(8,128)S(1)} fusion(f32[16,3072]{1,0:T(8,128)S(1)} %convolution_add_fusion, f32[192,3072]{1,0:T(8,128)} %param.22, f32[16,192]{1,0:T(8,128)S(1)} %fusion.26), kind=kOutput, calls=%fused_computation.5 | convolution fusion | flops 113273856 | bytes 2580480 | tf_op jit(solution)/shard_map/dot_general | solution.py:469
  148.5 3.5 %fusion.23 = f32[192,3072]{1,0:T(8,128)} fusion(f32[16,3072]{1,0:T(8,128)S(1)} %convolution_add_fusion, f32[16,192]{1,0:T(8,128)S(1)} %fusion.26), kind=kOutput, calls=%fused_computation.57 | convolution fusion | flops 113442816 | bytes 2568192 | tf_op jit(solution)/shard_map/dot_general | solution.py:468
  152.0 4.3 %fusion.27 = f32[192,4096]{1,0:T(8,128)} fusion(f32[16,192]{1,0:T(8,128)S(1)} %convolution_multiply_fusion, f32[16,4096]{1,0:T(8,128)S(1)} %copy-done.4), kind=kOutput, calls=%fused_computation.59 | convolution fusion | flops 150994944 | bytes 3420160 | tf_op jit(solution)/shard_map/dot_general | solution.py:472
  156.3 0.7 copy.39
  (43 shorter events, 1.7 us)
Async XLA Ops:
  0.6 1.9 %copy-start = (f32[192,4096]{1,0:T(8,128)S(1)}, f32[192,4096]{1,0:T(8,128)}, u32[]{:S(2)}) copy-start(f32[192,4096]{1,0:T(8,128)} %param.21) | copy-start | bytes 9437188
  0.6 29.2 %collective-permute-start = (bf16[256,3072]{1,0:T(8,128)(2,1)}, bf16[256,3072]{1,0:T(8,128)(2,1)}, u32[]{:S(2)}, u32[]{:S(2)}) collective-permute-start(bf16[256,3072]{1,0:T(8,128)(2,1)} %param.13), channel_id=1, source_target_pairs={{0,1},{1,0},{2,3},{3,2},{4,5},{5,4},{6,7},{7,6},{8,9},{9,8},{10,11... | collective-permute-start | bytes 4718600 | tf_op jit(solution)/shard_map/ppermute | solution.py:415
  1.2 28.5 %collective-permute-start.1 = (s32[256,2]{0,1:T(2,128)}, s32[256,2]{0,1:T(2,128)S(1)}, u32[]{:S(2)}, u32[]{:S(2)}) collective-permute-start(s32[256,2]{0,1:T(2,128)} %param.18), channel_id=1, source_target_pairs={{0,1},{1,0},{2,3},{3,2},{4,5},{5,4},{6,7},{7,6},{8,9},{9,8},{10,11... | collective-permute-start | bytes 6152 | tf_op jit(solution)/shard_map/ppermute | solution.py:416
  1.2 4.8 %copy-start.3 = (f32[192,3072]{1,0:T(8,128)S(1)}, f32[192,3072]{1,0:T(8,128)}, u32[]{:S(2)}) copy-start(f32[192,3072]{1,0:T(8,128)} %param.22) | copy-start | bytes 7077892
  2.5 27.1 %copy-start.7 = (s32[256,2]{0,1:T(2,128)S(1)}, s32[256,2]{0,1:T(2,128)}, u32[]{:S(2)}) copy-start(s32[256,2]{0,1:T(2,128)} %param.18) | copy-start | bytes 6148
  2.5 27.1 %copy-start.8 = (s32[16]{0:T(128)S(1)}, s32[16]{0:T(128)}, u32[]{:S(2)}) copy-start(s32[16]{0:T(128)} %param.19) | copy-start | bytes 196
  6.1 23.8 %copy-start.9 = (bf16[256,3072]{1,0:T(8,128)(2,1)S(1)}, bf16[256,3072]{1,0:T(8,128)(2,1)}, u32[]{:S(2)}) copy-start(bf16[256,3072]{1,0:T(8,128)(2,1)} %param.13) | copy-start | bytes 4718596
  32.4 0.7 copy-start.6
  33.1 2.7 %copy-start.2 = (bf16[528,3072]{1,0:T(8,128)(2,1)}, bf16[528,3072]{1,0:T(8,128)(2,1)S(1)}, u32[]{:S(2)}) copy-start(bf16[528,3072]{1,0:T(8,128)(2,1)S(1)} %pad_maximum_fusion.rows_ref) | copy-start | bytes 9732100
  142.2 9.8 %copy-start.4 = (f32[16,4096]{1,0:T(8,128)S(1)}, f32[16,4096]{1,0:T(8,128)}, u32[]{:S(2)}) copy-start(f32[16,4096]{1,0:T(8,128)} %param.20) | copy-start | bytes 786436
  144.8 12.3 %copy-start.1 = (f32[192,4096]{1,0:T(8,128)S(1)}, f32[192,4096]{1,0:T(8,128)}, u32[]{:S(2)}) copy-start(f32[192,4096]{1,0:T(8,128)} %param.21) | copy-start | bytes 9437188
  148.5 7.8 %copy-start.5 = (bf16[32,3072]{1,0:T(8,128)(2,1)S(1)}, bf16[32,3072]{1,0:T(8,128)(2,1)}, u32[]{:S(2)}) copy-start(bf16[32,3072]{1,0:T(8,128)(2,1)} %get-tuple-element.23) | copy-start | bytes 589828

commit v4 on v3

--- a/solution.py
+++ b/solution.py
@@ -214,10 +214,10 @@
             far_send.at[step], far_land.at[step], far_sems, 0, step, {"dp": goal(step, low)}
         )
 
+    for step in range(groups):
+        pair(step, True).start()
     for step in range(1, count):
         scatter(step).start()
-    for step in range(groups):
-        pair(step, True).start()
     for step in range(groups):
         pair(step, False).start()
     for step in range(groups):

time: 157 us -> 157 us (level)
  no operation moved by 1% of the time
where the time goes in v4:
time: 157 us
  Pallas kernels  124 us (79%)
  matrix products  20.3 us (13%)
  local copies, waits for them, and re-layouts  8.41 us (5%)
  other arithmetic  3.01 us (2%)
    pallas_call x1, Pallas kernels, run_experts(): pl.pallas_call(functools.partial(expert_kernel, tok_count), grid=(local_c...  68.9 us
    pallas_call x1, Pallas kernels, finish(): pl.pallas_call(functools.partial(finish_kernel, dp_count, halves), out_sh...  34.4 us
    pallas_call x1, Pallas kernels, sum_all(): pl.pallas_call(functools.partial(sum_kernel, groups), out_shape=jax.Shape...  20.6 us
    unnamed x27, local copies, waits for them, and re-layouts  4.97 us
    dot_general x1, matrix products, body(): grad_first = jnp.dot(grad_hidden.T, embed, precision=PRECISE)  4.31 us
    dot_general x1, matrix products, body(): lax.dot_general(grad_proj, w_second, (((1,), (1,)), ((), ())), precision=...  3.75 us
    dot_general x1, matrix products, body(): lax.dot_general(embed, w_first, (((1,), (1,)), ((), ())), precision=PRECISE)  3.51 us
    dot_general x1, matrix products, body(): grad_second = jnp.dot(activated.T, grad_proj, precision=PRECISE)  3.47 us
  transfers between devices with their start and end apart: 2, of which 0 were waited for; matrix products, arithmetic and copies ran while one was open for 5% of the time, Pallas kernels for 13%

profile of v4, /device:TPU:0, one launch (start us, length us, event | category | flops | bytes accessed | tf_op | source)
XLA Modules:
  0.0 157.0 jit_solution(17942844686243266366)
XLA Ops:
  0.6 0.5 collective-permute-start
  1.3 1.0 convert_reduce_fusion
  2.5 3.5 %fusion.26 = f32[16,192]{1,0:T(8,128)S(1)} fusion(f32[16,4096]{1,0:T(8,128)} %param.20, f32[192,4096]{1,0:T(8,128)S(1)} %copy-done), kind=kOutput, calls=%fused_computation.58 | convolution fusion | flops 150994944 | bytes 3420160 | tf_op jit(solution)/shard_map/dot_general | solution.py:425
  6.1 1.3 convolution_bitcast_fusion
  7.3 0.7 copy.29
  8.1 20.6 %shard_map.130 = f32[4,4,24,128]{3,2,1,0:T(8,128)} custom-call(f32[4,4,24,128]{3,2,1,0:T(8,128)} %bitcast.38), custom_call_target="tpu_custom_call" | custom-call | tf_op jit(solution)/shard_map/pallas_call | solution.py:119
  28.7 0.9 convert_element_type.21
  29.9 2.5 %maximum_select_fusion = bf16[512,3072]{1,0:T(8,128)(2,1)S(1)} fusion(bf16[256,3072]{1,0:T(8,128)(2,1)} %collective-permute-done, bf16[256,3072]{1,0:T(8,128)(2,1)S(1)} %copy-done.9, pred[512]{0:T(512)(128)(4,1)S(1)} %broadcast_compare_fusion, s32[512]{0:T(512)S(1)} %pad_add_fusion.1, s32[16]{0:T(128)S(1)} %copy-done.8, bf16[2,8,24,128]{3,2,1,0:T(8,128)(2,1)S(1)} %bitcast.40), kind=kOutput, calls=%fused_computation.3 | convolution fusion | flops 59793408 | bytes 6392384 | tf_op jit(solution)/shard_map/dot_general | solution.py:430
  32.6 0.5 copy-done.6
  33.1 1.0 multiply_reduce_fusion
  34.2 1.0 copy.26.gates_ref
  35.2 0.7 copy.27.doc_gates_ref
  35.9 68.9 %shard_map.131 = (bf16[512,3072]{1,0:T(8,128)(2,1)}, f32[16,3072]{1,0:T(8,128)}, f32[2,16,128]{2,1,0:T(8,128)}) custom-call(bf16[528,3072]{1,0:T(8,128)(2,1)} %copy-done.2, f32[2,512,1]{2,1,0:T(8,128)} %copy.26.gates_ref, f32[2,16,1]{2,1,0:T(8,128)} %copy.27.doc_gates_ref, bf16[16,3072]{1,0:T(8,128)(2,1)} %cot_ref.1, bf16[2,3072,2048]{2,1,0:T(8,128)(2,1)} %w_gate_ref.1, ...), custom_call_target="tpu_custom_call" | custom-call | tf_op jit(solution)/shard_map/pallas_call | solution.py:364
  104.8 1.0 copy.31
  105.7 0.8 slice_reduce_fusion
  106.6 0.3 dynamic_update_slice.3
  107.1 0.7 pad_maximum_fusion.1.x_ref
  107.8 34.4 %shard_map.132 = (f32[16,25,128]{2,1,0:T(8,128)}, bf16[32,3072]{1,0:T(8,128)(2,1)}) custom-call(f32[16,25,128]{2,1,0:T(8,128)} %pad_maximum_fusion.1.x_ref, bf16[2,8,32,3072]{3,2,1,0:T(8,128)(2,1)} %bitcast.35), custom_call_target="tpu_custom_call" | custom-call | tf_op jit(solution)/shard_map/pallas_call | solution.py:271
  142.2 0.9 slice_reduce_fusion.1
  143.1 0.9 slice.38
  144.7 3.8 %convolution_multiply_fusion = f32[16,192]{1,0:T(8,128)S(1)} fusion(f32[16,3072]{1,0:T(8,128)S(1)} %convolution_add_fusion, f32[192,3072]{1,0:T(8,128)} %param.22, f32[16,192]{1,0:T(8,128)S(1)} %fusion.26), kind=kOutput, calls=%fused_computation.5 | convolution fusion | flops 113273856 | bytes 2580480 | tf_op jit(solution)/shard_map/dot_general | solution.py:469
  148.5 3.5 %fusion.23 = f32[192,3072]{1,0:T(8,128)} fusion(f32[16,3072]{1,0:T(8,128)S(1)} %convolution_add_fusion, f32[16,192]{1,0:T(8,128)S(1)} %fusion.26), kind=kOutput, calls=%fused_computation.57 | convolution fusion | flops 113442816 | bytes 2568192 | tf_op jit(solution)/shard_map/dot_general | solution.py:468
  152.0 4.3 %fusion.27 = f32[192,4096]{1,0:T(8,128)} fusion(f32[16,192]{1,0:T(8,128)S(1)} %convolution_multiply_fusion, f32[16,4096]{1,0:T(8,128)S(1)} %copy-done.4), kind=kOutput, calls=%fused_computation.59 | convolution fusion | flops 150994944 | bytes 3420160 | tf_op jit(solution)/shard_map/dot_general | solution.py:472
  156.3 0.7 copy.39
  (43 shorter events, 1.7 us)
Async XLA Ops:
  0.6 1.9 %copy-start = (f32[192,4096]{1,0:T(8,128)S(1)}, f32[192,4096]{1,0:T(8,128)}, u32[]{:S(2)}) copy-start(f32[192,4096]{1,0:T(8,128)} %param.21) | copy-start | bytes 9437188
  0.6 29.2 %collective-permute-start = (bf16[256,3072]{1,0:T(8,128)(2,1)}, bf16[256,3072]{1,0:T(8,128)(2,1)}, u32[]{:S(2)}, u32[]{:S(2)}) collective-permute-start(bf16[256,3072]{1,0:T(8,128)(2,1)} %param.13), channel_id=1, source_target_pairs={{0,1},{1,0},{2,3},{3,2},{4,5},{5,4},{6,7},{7,6},{8,9},{9,8},{10,11... | collective-permute-start | bytes 4718600 | tf_op jit(solution)/shard_map/ppermute | solution.py:415
  1.2 28.5 %collective-permute-start.1 = (s32[256,2]{0,1:T(2,128)}, s32[256,2]{0,1:T(2,128)S(1)}, u32[]{:S(2)}, u32[]{:S(2)}) collective-permute-start(s32[256,2]{0,1:T(2,128)} %param.18), channel_id=1, source_target_pairs={{0,1},{1,0},{2,3},{3,2},{4,5},{5,4},{6,7},{7,6},{8,9},{9,8},{10,11... | collective-permute-start | bytes 6152 | tf_op jit(solution)/shard_map/ppermute | solution.py:416
  1.2 4.8 %copy-start.3 = (f32[192,3072]{1,0:T(8,128)S(1)}, f32[192,3072]{1,0:T(8,128)}, u32[]{:S(2)}) copy-start(f32[192,3072]{1,0:T(8,128)} %param.22) | copy-start | bytes 7077892
  2.5 27.1 %copy-start.7 = (s32[256,2]{0,1:T(2,128)S(1)}, s32[256,2]{0,1:T(2,128)}, u32[]{:S(2)}) copy-start(s32[256,2]{0,1:T(2,128)} %param.18) | copy-start | bytes 6148
  2.5 27.1 %copy-start.8 = (s32[16]{0:T(128)S(1)}, s32[16]{0:T(128)}, u32[]{:S(2)}) copy-start(s32[16]{0:T(128)} %param.19) | copy-start | bytes 196
  6.1 23.8 %copy-start.9 = (bf16[256,3072]{1,0:T(8,128)(2,1)S(1)}, bf16[256,3072]{1,0:T(8,128)(2,1)}, u32[]{:S(2)}) copy-start(bf16[256,3072]{1,0:T(8,128)(2,1)} %param.13) | copy-start | bytes 4718596
  32.4 0.7 copy-start.6
  33.1 2.7 %copy-start.2 = (bf16[528,3072]{1,0:T(8,128)(2,1)}, bf16[528,3072]{1,0:T(8,128)(2,1)S(1)}, u32[]{:S(2)}) copy-start(bf16[528,3072]{1,0:T(8,128)(2,1)S(1)} %pad_maximum_fusion.rows_ref) | copy-start | bytes 9732100
  142.2 9.8 %copy-start.4 = (f32[16,4096]{1,0:T(8,128)S(1)}, f32[16,4096]{1,0:T(8,128)}, u32[]{:S(2)}) copy-start(f32[16,4096]{1,0:T(8,128)} %param.20) | copy-start | bytes 786436
  144.7 12.3 %copy-start.1 = (f32[192,4096]{1,0:T(8,128)S(1)}, f32[192,4096]{1,0:T(8,128)}, u32[]{:S(2)}) copy-start(f32[192,4096]{1,0:T(8,128)} %param.21) | copy-start | bytes 9437188
  148.5 7.8 %copy-start.5 = (bf16[32,3072]{1,0:T(8,128)(2,1)S(1)}, bf16[32,3072]{1,0:T(8,128)(2,1)}, u32[]{:S(2)}) copy-start(bf16[32,3072]{1,0:T(8,128)(2,1)} %get-tuple-element.23) | copy-start | bytes 589828
